TPU v7x, 256 devices: a whole 4x4x8 slice. The times are simulated.
256 devices in a mesh: row: 8 (over y, core), col: 32 (over z, x).
Axes of the slice: x: 4, y: 4, z: 8, core: 2. Of those that a mesh axis runs over, the one named last changes fastest.
Arguments:
- covariance: float32 [8, 2048, 2, 8192], P(None, 'row', None, 'col'), as said below
Outputs:
- factored: float32 [8, 2048, 2, 8192], P(None, 'row', None, 'col')
Inputs may be any that keep to these rules, and one draw needn't show every extreme that they name: `covariance`: symmetric positive definite.
All inputs are finite; a program needn't handle non-finite values.
Results may differ from a plain program's by a relative error of at most 0.0001.
Values sent between devices are 32-bit elements; how exact they have to be, the bound alone decides.
No kernel may reach another device: no remote copies, remote signals or barrier semaphores. Data moves between devices by JAX's collectives and lax.ppermute only.
A program may use at most 64 MiB of HBM per device.

v0:
```python
import jax
import jax.numpy as jnp
import numpy as np
from jax import lax
from jax.sharding import PartitionSpec as P

PANELS = 3


def spread(array, axis, root):
    mine = lax.axis_index(axis) == root
    return lax.psum(jnp.where(mine, array, jnp.zeros_like(array)), axis)


def solve_right(factor, panel):
    return lax.linalg.triangular_solve(factor, panel, left_side=False, lower=True, transpose_a=True)


def shards(covariance):
    row_count = lax.axis_size("row")
    col_count = lax.axis_size("col")
    row_index = lax.axis_index("row")
    col_index = lax.axis_index("col")
    tile_rows = covariance.shape[0]
    tile_size = covariance.shape[1]
    tile_cols = covariance.shape[2]
    global_rows = jnp.arange(tile_rows, dtype=jnp.int32) * row_count + row_index
    global_cols = jnp.arange(tile_cols, dtype=jnp.int32) * col_count + col_index
    every_col = list(range(tile_cols))
    tiles = covariance
    for panel_index in range(PANELS):
        root_row = panel_index % row_count
        make_root_col = panel_index % col_count
        local_row = panel_index // row_count
        make_local_col = panel_index // col_count
        diag_raw = tiles[local_row, :, make_local_col, :]
        column_raw = tiles[:, :, make_local_col, :].reshape(tile_rows * tile_size, tile_size)
        diag_tile = spread(diag_raw, "row", root_row)
        make_factor = jnp.linalg.cholesky(diag_tile)
        solved = solve_right(make_factor, column_raw)
        make_row_panel = spread(solved, "col", make_root_col)
        make_panel_tiles = make_row_panel.reshape(tile_rows, tile_size, tile_size)
        wanted = (jnp.arange(tile_cols, dtype=jnp.int32) * col_count + col_index) // row_count
        picked = jnp.take(make_panel_tiles, wanted, axis=0)
        col_panel = spread(picked, "row", col_index % row_count)
        count = len(every_col)
        chosen_index = np.array(every_col, dtype=np.int32)
        col_part = col_panel[chosen_index].reshape(count * tile_size, tile_size)
        product = lax.dot_general(
            make_row_panel, col_part, (((1,), (1,)), ((), ())), precision=lax.Precision.HIGHEST
        )
        product = product.reshape(tile_rows, tile_size, count, tile_size)
        current = tiles[:, :, chosen_index, :]
        live_tiles = (global_rows > panel_index)[:, None, None, None] & (
            global_cols[chosen_index] > panel_index
        )[None, None, :, None]
        renewed = jnp.where(live_tiles, current - product, current)
        tiles = renewed
        write_tiles = tiles
        local_col = panel_index // col_count
        root_col = panel_index % col_count
        panel_tiles = make_row_panel.reshape(tile_rows, tile_size, tile_size)
        lower_tile = jnp.tril(make_factor)
        row_ids = global_rows[:, None, None]
        zero_tiles = jnp.zeros_like(panel_tiles)
        column_new = jnp.where(
            row_ids > panel_index,
            panel_tiles,
            jnp.where(row_ids == panel_index, lower_tile[None], zero_tiles),
        )
        column_old = write_tiles[:, :, local_col, :]
        write_tiles = write_tiles.at[:, :, local_col, :].set(
            jnp.where(col_index == root_col, column_new, column_old)
        )
        upper_tiles = (global_rows == panel_index)[:, None, None, None] & (
            global_cols > panel_index
        )[None, None, :, None]
        tiles = jnp.where(upper_tiles, jnp.zeros_like(write_tiles), write_tiles)
    return tiles


def solution(mesh):
    return jax.shard_map(
        shards,
        mesh=mesh,
        in_specs=(P(None, "row", None, "col"),),
        out_specs=P(None, "row", None, "col"),
        check_vma=False,
    )
```

profile of v0, /device:TPU:1, one launch (start us, length us, event | category | flops | bytes accessed | tf_op | source)
XLA Modules:
  0.0 1115.7 jit_solution(16226102619374735154)
XLA Ops:
  8.7 2.7 copy.31
  11.4 2.0 copy-done.2
  13.6 62.9 %all-reduce.11.cloned.1.call-done = f32[256,256]{0,1:T(8,128)} async-done(((f32[256,256]{0,1:T(8,128)}), f32[256,256]{0,1:T(8,128)}) %all-reduce.11.cloned.1.call-update) | async-done | bytes 262160 | tf_op jit(solution)/shard_map/psum | solution.py:12
  78.5 11.7 %cholesky.172 = f32[128,128]{1,0:T(8,128)S(1)} custom-call(f32[128,128]{1,0:T(8,128)S(1)} %cholesky.270), custom_call_target="Cholesky" | custom-call | tf_op jit(solution)/shard_map/jit(cholesky)/cholesky | solution.py:39
  90.3 9.8 custom-call.15
  100.6 11.7 %cholesky.189 = f32[128,128]{1,0:T(8,128)S(1)} custom-call(f32[128,128]{1,0:T(8,128)S(1)} %convolution_subtract_fusion.5), custom_call_target="Cholesky" | custom-call | tf_op jit(solution)/shard_map/jit(cholesky)/cholesky | solution.py:39
  114.5 4.3 while.9
  118.8 19.7 %custom-call.16 = f32[2,128,128]{1,2,0:T(8,128)S(1)} custom-call(f32[2,128,128]{2,1,0:T(8,128)S(1)} %get-tuple-element.64), custom_call_target="InvertDiagBlocksLowerTriangular" | custom-call | tf_op jit(solution)/shard_map/triangular_solve/custom-call.0 | solution.py:16
  139.5 1.8 convolution_subtract_fusion.2
  144.8 150.2 %all-reduce.13.cloned.1.call-done = f32[2048,256]{0,1:T(8,128)} async-done(((f32[2048,256]{0,1:T(8,128)}), f32[2048,256]{0,1:T(8,128)}) %all-reduce.13.cloned.1.call-update) | async-done | bytes 2097168 | tf_op jit(solution)/shard_map/psum | solution.py:12
  295.0 1.9 copy.68
  298.6 4.9 gather_fusion.1
  303.5 5.3 copy.32
  309.1 1.9 copy.41
  310.9 53.1 %all-reduce.15.cloned.1.call-done = f32[2,256,256]{2,1,0:T(8,128)} async-done(((f32[2,256,256]{2,1,0:T(8,128)}), f32[2,256,256]{2,1,0:T(8,128)}) %all-reduce.15.cloned.1.call-update) | async-done | bytes 524304 | tf_op jit(solution)/shard_map/psum | solution.py:12
  365.7 5.7 subtract_select_fusion.2
  372.5 2.0 copy-done.1
  376.9 2.3 copy.45
  379.2 60.4 %all-reduce.17.cloned.1.call-done = f32[256,256]{0,1:T(8,128)} async-done(((f32[256,256]{0,1:T(8,128)}), f32[256,256]{0,1:T(8,128)}) %all-reduce.17.cloned.1.call-update) | async-done | bytes 262160 | tf_op jit(solution)/shard_map/psum | solution.py:12
  441.7 11.7 %cholesky.206 = f32[128,128]{1,0:T(8,128)S(1)} custom-call(f32[128,128]{1,0:T(8,128)S(1)} %cholesky.273), custom_call_target="Cholesky" | custom-call | tf_op jit(solution)/shard_map/jit(cholesky)/cholesky | solution.py:39
  453.5 9.8 custom-call.17
  463.8 11.7 %cholesky.223 = f32[128,128]{1,0:T(8,128)S(1)} custom-call(f32[128,128]{1,0:T(8,128)S(1)} %convolution_subtract_fusion.4), custom_call_target="Cholesky" | custom-call | tf_op jit(solution)/shard_map/jit(cholesky)/cholesky | solution.py:39
  478.1 3.9 while.10
  482.0 19.8 %custom-call.18 = f32[2,128,128]{1,2,0:T(8,128)S(1)} custom-call(f32[2,128,128]{2,1,0:T(8,128)S(1)} %get-tuple-element.65), custom_call_target="InvertDiagBlocksLowerTriangular" | custom-call | tf_op jit(solution)/shard_map/triangular_solve/custom-call.0 | solution.py:16
  502.9 1.8 convolution_subtract_fusion.1
  507.5 151.0 %all-reduce.19.cloned.1.call-done = f32[2048,256]{0,1:T(8,128)} async-done(((f32[2048,256]{0,1:T(8,128)}), f32[2048,256]{0,1:T(8,128)}) %all-reduce.19.cloned.1.call-update) | async-done | bytes 2097168 | tf_op jit(solution)/shard_map/psum | solution.py:12
  658.5 1.9 copy.69
  662.1 4.9 gather_fusion.3
  667.1 1.8 copy.51
  669.0 58.5 %all-reduce.21.cloned.1.call-done = f32[2,256,256]{2,1,0:T(8,128)} async-done(((f32[2,256,256]{2,1,0:T(8,128)}), f32[2,256,256]{2,1,0:T(8,128)}) %all-reduce.21.cloned.1.call-update) | async-done | bytes 524304 | tf_op jit(solution)/shard_map/psum | solution.py:12
  729.1 5.7 subtract_select_fusion.1
  736.0 2.0 copy-done
  740.4 2.1 copy.54
  742.4 60.6 %all-reduce.23.cloned.1.call-done = f32[256,256]{0,1:T(8,128)} async-done(((f32[256,256]{0,1:T(8,128)}), f32[256,256]{0,1:T(8,128)}) %all-reduce.23.cloned.1.call-update) | async-done | bytes 262160 | tf_op jit(solution)/shard_map/psum | solution.py:12
  805.1 11.7 %cholesky.240 = f32[128,128]{1,0:T(8,128)S(1)} custom-call(f32[128,128]{1,0:T(8,128)S(1)} %cholesky.276), custom_call_target="Cholesky" | custom-call | tf_op jit(solution)/shard_map/jit(cholesky)/cholesky | solution.py:39
  816.9 9.8 custom-call.19
  827.2 11.7 %cholesky.257 = f32[128,128]{1,0:T(8,128)S(1)} custom-call(f32[128,128]{1,0:T(8,128)S(1)} %convolution_subtract_fusion.3), custom_call_target="Cholesky" | custom-call | tf_op jit(solution)/shard_map/jit(cholesky)/cholesky | solution.py:39
  841.6 3.9 while.11
  845.4 19.9 %custom-call.20 = f32[2,128,128]{1,2,0:T(8,128)S(1)} custom-call(f32[2,128,128]{2,1,0:T(8,128)S(1)} %get-tuple-element.66), custom_call_target="InvertDiagBlocksLowerTriangular" | custom-call | tf_op jit(solution)/shard_map/triangular_solve/custom-call.0 | solution.py:16
  866.5 1.8 convolution_subtract_fusion
  871.0 151.0 %all-reduce.25.cloned.1.call-done = f32[2048,256]{0,1:T(8,128)} async-done(((f32[2048,256]{0,1:T(8,128)}), f32[2048,256]{0,1:T(8,128)}) %all-reduce.25.cloned.1.call-update) | async-done | bytes 2097168 | tf_op jit(solution)/shard_map/psum | solution.py:12
  1022.0 1.9 copy.70
  1025.5 4.9 gather_fusion.5
  1030.6 1.8 copy.60
  1032.4 58.6 %all-reduce.27.cloned.1.call-done = f32[2,256,256]{2,1,0:T(8,128)} async-done(((f32[2,256,256]{2,1,0:T(8,128)}), f32[2,256,256]{2,1,0:T(8,128)}) %all-reduce.27.cloned.1.call-update) | async-done | bytes 524304 | tf_op jit(solution)/shard_map/psum | solution.py:12
  1092.6 5.7 subtract_select_fusion
  1099.0 2.6 broadcast_select_fusion.1
  1101.6 7.2 copy.61
  (145 shorter events, 55.1 us)
Async XLA Ops:
  6.5 69.9 %all-reduce.11.cloned.1.call-start = ((), (), s32[]{:S(2)}) async-start(), calls=%async_computation | async-start | bytes 524288 | tf_op jit(solution)/shard_map/psum | solution.py:12
  8.7 286.4 %all-reduce.13.cloned.1.call-start = ((), (), s32[]{:S(2)}) async-start(), calls=%async_computation.1 | async-start | bytes 4194304 | tf_op jit(solution)/shard_map/psum | solution.py:12
  11.4 2.0 copy-start.2
  143.9 220.1 %all-reduce.15.cloned.1.call-start = ((), (), s32[]{:S(2)}) async-start(), calls=%async_computation.2 | async-start | bytes 1048576 | tf_op jit(solution)/shard_map/psum | solution.py:12
  298.5 141.1 %all-reduce.17.cloned.1.call-start = ((), (), s32[]{:S(2)}) async-start(), calls=%async_computation.3 | async-start | bytes 524288 | tf_op jit(solution)/shard_map/psum | solution.py:12
  365.7 5.7 copy-start.6
  372.5 2.0 copy-start.1
  375.3 283.2 %all-reduce.19.cloned.1.call-start = ((), (), s32[]{:S(2)}) async-start(), calls=%async_computation.4 | async-start | bytes 4194304 | tf_op jit(solution)/shard_map/psum | solution.py:12
  375.3 1.6 slice-start.1
  379.2 122.7 %copy-start.4 = (f32[8,256,1,256]{3,1,0,2:T(8,128)S(1)}, f32[8,256,1,256]{3,1,0,2:T(8,128)}, u32[]{:S(2)}) copy-start(f32[8,256,1,256]{3,1,0,2:T(8,128)} %copy.45) | copy-start | bytes 6291460
  507.3 220.1 %all-reduce.21.cloned.1.call-start = ((), (), s32[]{:S(2)}) async-start(), calls=%async_computation.5 | async-start | bytes 1048576 | tf_op jit(solution)/shard_map/psum | solution.py:12
  661.9 141.1 %all-reduce.23.cloned.1.call-start = ((), (), s32[]{:S(2)}) async-start(), calls=%async_computation.6 | async-start | bytes 524288 | tf_op jit(solution)/shard_map/psum | solution.py:12
  729.1 5.7 copy-start.7
  736.0 2.0 copy-start
  738.7 283.3 %all-reduce.25.cloned.1.call-start = ((), (), s32[]{:S(2)}) async-start(), calls=%async_computation.7 | async-start | bytes 4194304 | tf_op jit(solution)/shard_map/psum | solution.py:12
  738.8 1.6 slice-start
  742.4 122.9 %copy-start.3 = (f32[8,256,1,256]{3,1,0,2:T(8,128)S(1)}, f32[8,256,1,256]{3,1,0,2:T(8,128)}, u32[]{:S(2)}) copy-start(f32[8,256,1,256]{3,1,0,2:T(8,128)} %copy.54) | copy-start | bytes 6291460
  870.9 220.1 %all-reduce.27.cloned.1.call-start = ((), (), s32[]{:S(2)}) async-start(), calls=%async_computation.8 | async-start | bytes 1048576 | tf_op jit(solution)/shard_map/psum | solution.py:12
  1092.6 5.7 copy-start.5
Sparse Core Ops, SparseCore 0:
  9.7 66.7 all-reduce.10
  144.0 150.9 all-reduce.12
  298.6 65.3 all-reduce.14
  375.4 64.1 all-reduce.16
  507.5 150.9 all-reduce.18
  662.1 65.3 all-reduce.20
  738.8 64.1 all-reduce.22
  871.0 150.9 all-reduce.24
  1025.6 65.3 all-reduce.26
where the time goes:
time: 1130 us; the launch traced here: 1120 us
  waiting for transfers between devices  806 us (71%)
  other arithmetic  181 us (16%)
  local copies, waits for them, and re-layouts  79 us (7%)
  matrix products  30.4 us (3%)
  between operations  18.1 us (2%)
    psum x9, waiting for transfers between devices, spread(): return lax.psum(jnp.where(mine, array, jnp.zeros_like(array)), axis)  806 us
    another operation x20, other arithmetic, shards(): make_factor = jnp.linalg.cholesky(diag_tile)  103 us
    another operation x7, other arithmetic, solve_right(): lax.linalg.triangular_solve(factor, panel, left_side=False, lower=True, t...  59.5 us
  transfers between devices with their start and end apart: 9, of which 9 were waited for; matrix products, arithmetic and copies ran while one was open for 3% of the time, Pallas kernels for 0%

commit v1 on v0

v1 whole, which is shorter than its diff:
```python
import jax
import jax.numpy as jnp
from jax import lax
from jax.sharding import PartitionSpec as P

NB = 256
PANELS = 3
K = PANELS * NB
NY, NX, NZ = 4, 4, 8
HI = lax.Precision.HIGHEST


def row_perm(shift):
    return [(y * 2 + core, ((y + shift) % NY) * 2 + core) for y in range(NY) for core in range(2)]


def x_perm(shift, limit):
    return [(z * NX + x, z * NX + (x + shift) % NX) for z in range(NZ) for x in range(limit)]


def z_perm(step):
    pairs = [(z, z + step) for z in range(0, NZ, 2 * step)]
    return [(a * NX + x, b * NX + x) for a, b in pairs for x in range(PANELS)]


def gather_row(block, y_index, core_index):
    stack = [block] + [lax.ppermute(block, "row", row_perm(s)) for s in (1, 2, 3)]
    mine = jnp.take(jnp.stack(stack), (y_index - jnp.arange(NY)) % NY, axis=0)
    swap = [(2 * y + core, 2 * y + 1 - core) for y in range(NY) for core in range(2)]
    other = lax.ppermute(mine, "row", swap)
    first = jnp.where(core_index == 0, mine, other)
    second = jnp.where(core_index == 0, other, mine)
    return jnp.stack([first, second], axis=1).reshape((2 * NY,) + block.shape)


def shards(cov):
    row = lax.axis_index("row")
    col = lax.axis_index("col")
    y_index, core_index = row // 2, row % 2
    z_index, x_index = col // NX, col % NX
    top = cov[0].reshape(NB, 2 * NB)
    piece = lax.all_to_all(top, "row", 0, 0, tiled=True)[: K // 8]

    turn = [
        (rr * 32 + g * 8 + m, m * 32 + g * 8 + rr)
        for rr in range(8)
        for g in range(4)
        for m in range(8)
    ]
    turned = lax.ppermute(piece, ("row", "col"), turn)
    rows_t = lax.all_gather(turned, "col", axis=0).reshape(4, K, 2 * NB)

    part = piece[:, :NB]
    for step in (4, 2, 1):
        got = lax.ppermute(part, "col", z_perm(step))
        part = jnp.where(z_index % (2 * step) == step, got, part)
    around = [part] + [lax.ppermute(part, "col", x_perm(s, PANELS)) for s in (1, 2, 3)]
    wide = jnp.take(jnp.stack(around), (x_index - jnp.arange(PANELS)) % NX, axis=0)
    wide = wide.transpose(1, 0, 2).reshape(K // 8, K)
    diag = gather_row(wide, y_index, core_index)
    diag = diag.reshape(8, PANELS, 32, K).transpose(1, 0, 2, 3).reshape(K, K)

    mine = gather_row(piece, y_index, core_index).reshape(K, 2 * NB)

    low = jnp.linalg.cholesky(diag, symmetrize_input=False)
    inv = lax.linalg.triangular_solve(low, jnp.eye(K, dtype=jnp.float32), left_side=True, lower=True)
    inv_p = inv.reshape(K, PANELS, 8, 32).transpose(0, 2, 1, 3).reshape(K, K)
    half = jnp.dot(inv_p, mine, precision=HI)
    weights = lax.dot_general(inv_p, half, (((0,), (0,)), ((), ())), precision=HI)
    panel = jnp.minimum(col, PANELS - 1)
    solve = lax.dynamic_slice(inv_p, (panel * NB, 0), (NB, K)).T
    in_panel = col < PANELS
    left = jnp.where(in_panel, -solve, weights[:, :NB])
    weights = jnp.concatenate([left, weights[:, NB:]], axis=1)

    product = lax.dot_general(rows_t, weights, (((1,), (0,)), ((), ())), precision=HI)
    product = product.reshape(4, 2, NB, 2, NB).transpose(1, 0, 2, 3, 4).reshape(8, NB, 2, NB)
    drop = in_panel & (jnp.arange(2) == 0)
    out = jnp.where(drop[None, None, :, None], 0.0, cov) - product
    tile = lax.dynamic_slice(low, (jnp.minimum(row, PANELS - 1) * NB, panel * NB), (NB, NB))
    tile = jnp.where(in_panel, tile, 0.0)
    first = jnp.stack([tile, jnp.zeros_like(tile)], axis=1)
    is_top = (jnp.arange(8) == 0) & (row < PANELS)
    return jnp.where(is_top[:, None, None, None], first[None], out)


def solution(mesh):
    return jax.shard_map(
        shards,
        mesh=mesh,
        in_specs=(P(None, "row", None, "col"),),
        out_specs=P(None, "row", None, "col"),
        check_vma=False,
    )
```

time: 1130 us -> 411 us (0.36)
  the two profiles are of different devices: /device:TPU:1 before, /device:TPU:249 now
where the time goes in v1:
time: 411 us; the launch traced here: 403 us
  other arithmetic  205 us (50%)
  local copies, waits for them, and re-layouts  52.5 us (13%)
  matrix products  49.3 us (12%)
  waiting for transfers between devices  40.6 us (10%)
  starting transfers between devices  38.1 us (9%)
  between operations  18 us (4%)
    another operation x22, other arithmetic, shards(): low = jnp.linalg.cholesky(diag, symmetrize_input=False)  123 us
    another operation x3, other arithmetic, shards(): lax.linalg.triangular_solve(low, jnp.eye(K, dtype=jnp.float32), left_side...  62.3 us
    another operation x18, local copies, waits for them, and re-layouts  20.6 us
    another operation x11, matrix products, shards(): lax.linalg.triangular_solve(low, jnp.eye(K, dtype=jnp.float32), left_side...  17.4 us
    ppermute x3, waiting for transfers between devices, shards(): got = lax.ppermute(part, 'col', z_perm(step))  15 us
    ppermute x2, starting transfers between devices, gather_row(): other = lax.ppermute(mine, 'row', swap)  14.4 us
    dot_general x1, matrix products, shards(): lax.dot_general(rows_t, weights, (((1,), (0,)), ((), ())), precision=HI)  13.9 us
    ppermute x1, waiting for transfers between devices, shards(): turned = lax.ppermute(piece, ('row', 'col'), turn)  12.4 us
  transfers between devices with their start and end apart: 17, of which 7 were waited for; matrix products, arithmetic and copies ran while one was open for 65% of the time, Pallas kernels for 0%

profile of v1, /device:TPU:249, one launch (start us, length us, event | category | flops | bytes accessed | tf_op | source)
XLA Modules:
  0.0 403.4 jit_solution(17805091120070030073)
XLA Ops:
  9.0 5.0 %all-to-all-start = ((f32[8,32,512]{2,1,0:T(8,128)}), f32[8,32,512]{2,1,0:T(8,128)S(1)}, u32[]{:S(2)}, u32[]{:S(2)}) async-start(f32[8,32,512]{2,1,0:T(8,128)} %all_to_all.8), calls=%async_computation | async-start | bytes 1048576 | tf_op jit(solution)/shard_map/all_to_all | solution.py:42
  14.0 7.7 %all-to-all-done = f32[8,32,512]{2,1,0:T(8,128)S(1)} async-done(((f32[8,32,512]{2,1,0:T(8,128)}), f32[8,32,512]{2,1,0:T(8,128)S(1)}, u32[]{:S(2)}, u32[]{:S(2)}) %all-to-all-start) | async-done | bytes 524320 | tf_op jit(solution)/shard_map/all_to_all | solution.py:42
  24.5 15.0 %collective-permute-done.2 = f32[96,256]{1,0:T(8,128)S(1)} collective-permute-done((f32[96,256]{1,0:T(8,128)S(1)}, f32[96,256]{1,0:T(8,128)S(1)}, u32[]{:S(2)}, u32[]{:S(2)}) %collective-permute-start.2) | collective-permute-done | bytes 98336 | tf_op jit(solution)/shard_map/ppermute | solution.py:55
  39.5 3.1 collective-permute-start.3
  42.7 3.5 collective-permute-start.4
  46.1 1.9 collective-permute-start.5
  48.1 1.9 collective-permute-start.10
  53.0 1.9 collective-permute-start.6
  56.1 1.8 collective-permute-done.12
  59.7 11.9 %collective-permute-start.13 = (f32[4,96,512]{2,1,0:T(8,128)}, f32[4,96,512]{2,1,0:T(8,128)}, u32[]{:S(2)}, u32[]{:S(2)}) collective-permute-start(f32[4,96,512]{2,1,0:T(8,128)} %broadcast_select_fusion.1), channel_id=1, source_target_pairs={{0,32},{32,0},{64,96},{96,64},{128,160},{160,128},{192,224},{224,1... | collective-permute-start | bytes 2359304 | tf_op jit(solution)/shard_map/ppermute | solution.py:30
  72.0 1.9 collective-permute-done.8
  77.6 2.5 collective-permute-start.9
  80.1 2.1 collective-permute-start.14
  82.3 12.4 %collective-permute-done.14 = f32[96,512]{1,0:T(8,128)S(1)} collective-permute-done((f32[96,512]{1,0:T(8,128)S(1)}, f32[96,512]{1,0:T(8,128)S(1)}, u32[]{:S(2)}, u32[]{:S(2)}) %collective-permute-start.14) | collective-permute-done | bytes 196640 | tf_op jit(solution)/shard_map/ppermute | solution.py:50
  96.4 1.6 fusion.23
  103.1 11.7 %cholesky.165 = f32[128,128]{1,0:T(8,128)S(1)} custom-call(f32[128,128]{1,0:T(8,128)S(1)} %cholesky.424), custom_call_target="Cholesky" | custom-call | tf_op jit(solution)/shard_map/jit(cholesky)/cholesky | solution.py:65
  115.0 9.8 %custom-call.46 = f32[1,128,128]{1,2,0:T(8,128)S(1)} custom-call(f32[1,128,128]{2,1,0:T(8,128)S(1)} %get-tuple-element.58), custom_call_target="InvertDiagBlocksLowerTriangular" | custom-call | tf_op jit(solution)/shard_map/jit(cholesky)/cholesky | solution.py:65
  127.6 12.1 %cholesky.188 = f32[128,128]{1,0:T(8,128)S(1)} custom-call(f32[128,128]{1,0:T(8,128)S(1)} %cholesky.428), custom_call_target="Cholesky" | custom-call | tf_op jit(solution)/shard_map/jit(cholesky)/cholesky | solution.py:65
  139.7 9.8 %custom-call.47 = f32[1,128,128]{1,2,0:T(8,128)S(1)} custom-call(f32[1,128,128]{2,1,0:T(8,128)S(1)} %get-tuple-element.55), custom_call_target="InvertDiagBlocksLowerTriangular" | custom-call | tf_op jit(solution)/shard_map/jit(cholesky)/cholesky | solution.py:65
  151.5 11.7 %cholesky.354 = f32[128,128]{1,0:T(8,128)S(1)} custom-call(f32[128,128]{1,0:T(8,128)S(1)} %cholesky.433), custom_call_target="Cholesky" | custom-call | tf_op jit(solution)/shard_map/jit(cholesky)/cholesky | solution.py:65
  163.2 9.8 %custom-call.48 = f32[1,128,128]{1,2,0:T(8,128)S(1)} custom-call(f32[1,128,128]{2,1,0:T(8,128)S(1)} %get-tuple-element.52), custom_call_target="InvertDiagBlocksLowerTriangular" | custom-call | tf_op jit(solution)/shard_map/jit(cholesky)/cholesky | solution.py:65
  173.4 1.6 convolution_subtract_fusion.6
  175.0 11.9 %cholesky.373 = f32[128,128]{1,0:T(8,128)S(1)} custom-call(f32[128,128]{1,0:T(8,128)S(1)} %cholesky.438), custom_call_target="Cholesky" | custom-call | tf_op jit(solution)/shard_map/jit(cholesky)/cholesky | solution.py:65
  186.9 9.8 %custom-call.49 = f32[1,128,128]{1,2,0:T(8,128)S(1)} custom-call(f32[1,128,128]{2,1,0:T(8,128)S(1)} %get-tuple-element.49), custom_call_target="InvertDiagBlocksLowerTriangular" | custom-call | tf_op jit(solution)/shard_map/jit(cholesky)/cholesky | solution.py:65
  198.5 11.7 %cholesky.392 = f32[128,128]{1,0:T(8,128)S(1)} custom-call(f32[128,128]{1,0:T(8,128)S(1)} %cholesky.443), custom_call_target="Cholesky" | custom-call | tf_op jit(solution)/shard_map/jit(cholesky)/cholesky | solution.py:65
  210.2 9.8 %custom-call.50 = f32[1,128,128]{1,2,0:T(8,128)S(1)} custom-call(f32[1,128,128]{2,1,0:T(8,128)S(1)} %get-tuple-element.46), custom_call_target="InvertDiagBlocksLowerTriangular" | custom-call | tf_op jit(solution)/shard_map/jit(cholesky)/cholesky | solution.py:65
  221.6 11.9 %cholesky.410 = f32[128,128]{1,0:T(8,128)S(1)} custom-call(f32[128,128]{1,0:T(8,128)S(1)} %convolution_subtract_fusion.8), custom_call_target="Cholesky" | custom-call | tf_op jit(solution)/shard_map/jit(cholesky)/cholesky | solution.py:65
  240.5 2.5 fusion.1
  243.0 20.7 %while.1 = (s32[]{:T(128)}, f32[768,768]{1,0:T(8,128)}, s32[6,2]{0,1:T(2,128)S(1)}, f32[6,128,128]{2,1,0:T(8,128)}, s32[]{:T(128)}) while((s32[]{:T(128)}, f32[768,768]{1,0:T(8,128)}, s32[6,2]{0,1:T(2,128)S(1)}, f32[6,128,128]{2,1,0:T(8,128)}, s32[]{:T(128)}) %tuple.45), condition=%wide.while_cond, body=%wide.while_body.sunk | while | flops 2 | bytes 132705 | solution.py:66
  243.6 2.9 bitcast_dynamic-update-slice_fusion.2
  247.2 2.8 bitcast_dynamic-update-slice_fusion.2
  250.6 2.8 bitcast_dynamic-update-slice_fusion.2
  254.0 2.8 bitcast_dynamic-update-slice_fusion.2
  257.5 2.8 bitcast_dynamic-update-slice_fusion.2
  260.9 2.8 bitcast_dynamic-update-slice_fusion.2
  263.7 59.8 %custom-call.51 = f32[6,128,128]{1,2,0:T(8,128)S(1)} custom-call(f32[6,128,128]{2,1,0:T(8,128)} %get-tuple-element.12), custom_call_target="InvertDiagBlocksLowerTriangular" | custom-call | tf_op jit(solution)/shard_map/triangular_solve | solution.py:66
  323.4 1.9 constant_dynamic-update-slice_fusion.4
  330.9 1.8 convolution_subtract_fusion.1
  334.0 2.0 fusion.12
  337.3 2.3 convolution_subtract_fusion
  340.9 3.4 copy.18
  344.3 1.8 copy.19
  348.9 3.9 fusion.65
  352.8 4.4 %fusion.66 = f32[768,512]{0,1:T(8,128)S(1)} fusion(f32[768,768]{0,1:T(8,128)S(1)} %bitcast.138, f32[768,512]{1,0:T(8,128)S(1)} %fusion.65), kind=kOutput, calls=%fused_computation.172 | convolution fusion | flops 3623878656 | bytes 5505024 | tf_op jit(solution)/shard_map/dot_general | solution.py:69
  357.4 13.9 %convolution_bitcast_fusion = f32[4,512,512]{1,2,0:T(8,128)} fusion(f32[4,768,512]{2,1,0:T(8,128)} %bitcast.142, f32[768,256]{0,1:T(8,128)S(1)} %get-tuple-element.28, f32[768,256]{0,1:T(8,128)S(1)} %get-tuple-element.27), kind=kOutput, calls=%fused_computation.12 | convolution fusion | flops 9664069632 | bytes 12058624 | tf_op jit(solution)/shard_map/dot_general | solution.py:76
  371.3 5.9 %reshape.201 = f32[4,2,256,2,256]{2,1,4,3,0:T(2,128)} reshape(f32[4,512,512]{1,2,0:T(8,128)} %convolution_bitcast_fusion) | data formatting | bytes 8388608 | tf_op jit(solution)/shard_map/reshape | solution.py:77
  377.2 11.0 %copy.22 = f32[2,4,256,2,256]{4,3,2,1,0:T(2,128)} copy(f32[2,4,256,2,256]{2,0,4,3,1:T(2,128)} %bitcast.139) | data formatting | bytes 8388608 | tf_op jit(solution)/shard_map/transpose | solution.py:77
  388.1 8.2 %fusion = f32[8,256,2,256]{3,2,1,0:T(2,128)} fusion(f32[2,4,256,2,256]{4,3,2,1,0:T(2,128)} %copy.22, f32[8,256,2,256]{3,2,1,0:T(2,128)} %param.1, pred[2]{0:T(512)(128)(4,1)S(1)} %compare_and_fusion, pred[8]{0:T(512)(128)(4,1)S(1)} %compare_and_fusion.3, f32[256,2,256]{2,1,0:T(2,128)S(1)} %stack.79.clone), kind=kLoop, calls=%fused_computation.6 | loop fusion | flops 3145728 | bytes 13107210 | tf_op jit(solution)/shard_map/jit(_where)/select_n | solution.py:84
  (125 shorter events, 49.9 us)
Async XLA Ops:
  9.0 12.8 %all-to-all-start = ((f32[8,32,512]{2,1,0:T(8,128)}), f32[8,32,512]{2,1,0:T(8,128)S(1)}, u32[]{:S(2)}, u32[]{:S(2)}) async-start(f32[8,32,512]{2,1,0:T(8,128)} %all_to_all.8), calls=%async_computation | async-start | bytes 1048576 | tf_op jit(solution)/shard_map/all_to_all | solution.py:42
  14.0 343.4 %all-gather.3.cloned.1.call-start = ((), (), s32[]{:S(2)}) async-start(), calls=%async_computation.1 | async-start | bytes 6488064 | tf_op jit(solution)/shard_map/all_gather | solution.py:51
  21.8 0.7 collective-permute-start
  22.5 0.7 collective-permute-start.1
  23.2 16.3 %collective-permute-start.2 = (f32[96,256]{1,0:T(8,128)S(1)}, f32[96,256]{1,0:T(8,128)S(1)}, u32[]{:S(2)}, u32[]{:S(2)}) collective-permute-start(f32[96,256]{1,0:T(8,128)S(1)} %broadcast_select_fusion.3), channel_id=1, source_target_pairs={{0,4},{1,5},{2,6},{8,12},{9,13},{10,14},{16,20},{17,21},{18,22},{2... | collective-permute-start | bytes 294920 | tf_op jit(solution)/shard_map/ppermute | solution.py:55
  39.5 10.5 %collective-permute-start.3 = (f32[96,256]{1,0:T(8,128)S(1)}, f32[96,256]{1,0:T(8,128)S(1)}, u32[]{:S(2)}, u32[]{:S(2)}) collective-permute-start(f32[96,256]{1,0:T(8,128)S(1)} %broadcast_select_fusion.4), channel_id=1, source_target_pairs={{0,1},{1,2},{2,3},{4,5},{5,6},{6,7},{8,9},{9,10},{10,11},{12,13},{... | collective-permute-start | bytes 294920 | tf_op jit(solution)/shard_map/ppermute | solution.py:57
  42.7 8.2 %collective-permute-start.4 = (f32[96,256]{1,0:T(8,128)S(1)}, f32[96,256]{1,0:T(8,128)S(1)}, u32[]{:S(2)}, u32[]{:S(2)}) collective-permute-start(f32[96,256]{1,0:T(8,128)S(1)} %broadcast_select_fusion.4), channel_id=1, source_target_pairs={{0,2},{1,3},{2,0},{4,6},{5,7},{6,4},{8,10},{9,11},{10,8},{12,14},{... | collective-permute-start | bytes 294920 | tf_op jit(solution)/shard_map/ppermute | solution.py:57
  46.1 6.2 %collective-permute-start.5 = (f32[96,256]{1,0:T(8,128)S(1)}, f32[96,256]{1,0:T(8,128)S(1)}, u32[]{:S(2)}, u32[]{:S(2)}) collective-permute-start(f32[96,256]{1,0:T(8,128)S(1)} %broadcast_select_fusion.4), channel_id=1, source_target_pairs={{0,3},{1,0},{2,1},{4,7},{5,4},{6,5},{8,11},{9,8},{10,9},{12,15},{1... | collective-permute-start | bytes 294920 | tf_op jit(solution)/shard_map/ppermute | solution.py:57
  48.1 7.1 %collective-permute-start.10 = (f32[96,512]{1,0:T(8,128)S(1)}, f32[96,512]{1,0:T(8,128)S(1)}, u32[]{:S(2)}, u32[]{:S(2)}) collective-permute-start(f32[96,512]{1,0:T(8,128)S(1)} %bitcast.153), channel_id=1, source_target_pairs={{0,64},{32,96},{64,128},{96,160},{128,192},{160,224},{192,0},{224,... | collective-permute-start | bytes 589832 | tf_op jit(solution)/shard_map/ppermute | solution.py:27
  50.0 6.1 %collective-permute-start.11 = (f32[96,512]{1,0:T(8,128)S(1)}, f32[96,512]{1,0:T(8,128)S(1)}, u32[]{:S(2)}, u32[]{:S(2)}) collective-permute-start(f32[96,512]{1,0:T(8,128)S(1)} %bitcast.154), channel_id=1, source_target_pairs={{0,128},{32,160},{64,192},{96,224},{128,0},{160,32},{192,64},{224,... | collective-permute-start | bytes 589832 | tf_op jit(solution)/shard_map/ppermute | solution.py:27
  50.1 7.8 %collective-permute-start.12 = (f32[96,512]{1,0:T(8,128)S(1)}, f32[96,512]{1,0:T(8,128)S(1)}, u32[]{:S(2)}, u32[]{:S(2)}) collective-permute-start(f32[96,512]{1,0:T(8,128)S(1)} %bitcast.155), channel_id=1, source_target_pairs={{0,192},{32,224},{64,0},{96,32},{128,64},{160,96},{192,128},{224,1... | collective-permute-start | bytes 589832 | tf_op jit(solution)/shard_map/ppermute | solution.py:27
  53.0 18.9 %collective-permute-start.6 = (f32[96,768]{1,0:T(8,128)S(1)}, f32[96,768]{1,0:T(8,128)S(1)}, u32[]{:S(2)}, u32[]{:S(2)}) collective-permute-start(f32[96,768]{1,0:T(8,128)S(1)} %bitcast.162), channel_id=1, source_target_pairs={{0,64},{32,96},{64,128},{96,160},{128,192},{160,224},{192,0},{224,... | collective-permute-start | bytes 884744 | tf_op jit(solution)/shard_map/ppermute | solution.py:27
  54.9 17.1 %collective-permute-start.7 = (f32[96,768]{1,0:T(8,128)S(1)}, f32[96,768]{1,0:T(8,128)S(1)}, u32[]{:S(2)}, u32[]{:S(2)}) collective-permute-start(f32[96,768]{1,0:T(8,128)S(1)} %bitcast.163), channel_id=1, source_target_pairs={{0,128},{32,160},{64,192},{96,224},{128,0},{160,32},{192,64},{224,... | collective-permute-start | bytes 884744 | tf_op jit(solution)/shard_map/ppermute | solution.py:27
  55.2 18.6 %collective-permute-start.8 = (f32[96,768]{1,0:T(8,128)S(1)}, f32[96,768]{1,0:T(8,128)S(1)}, u32[]{:S(2)}, u32[]{:S(2)}) collective-permute-start(f32[96,768]{1,0:T(8,128)S(1)} %bitcast.164), channel_id=1, source_target_pairs={{0,192},{32,224},{64,0},{96,32},{128,64},{160,96},{192,128},{224,1... | collective-permute-start | bytes 884744 | tf_op jit(solution)/shard_map/ppermute | solution.py:27
  59.7 38.4 %collective-permute-start.13 = (f32[4,96,512]{2,1,0:T(8,128)}, f32[4,96,512]{2,1,0:T(8,128)}, u32[]{:S(2)}, u32[]{:S(2)}) collective-permute-start(f32[4,96,512]{2,1,0:T(8,128)} %broadcast_select_fusion.1), channel_id=1, source_target_pairs={{0,32},{32,0},{64,96},{96,64},{128,160},{160,128},{192,224},{224,1... | collective-permute-start | bytes 2359304 | tf_op jit(solution)/shard_map/ppermute | solution.py:30
  72.0 1.9 copy-start.4
  72.0 1.9 copy-start.5
  73.9 0.7 copy-start.6
  77.6 23.2 %collective-permute-start.9 = (f32[4,96,768]{2,1,0:T(8,128)}, f32[4,96,768]{2,1,0:T(8,128)S(1)}, u32[]{:S(2)}, u32[]{:S(2)}) collective-permute-start(f32[4,96,768]{2,1,0:T(8,128)} %broadcast_select_fusion), channel_id=1, source_target_pairs={{0,32},{32,0},{64,96},{96,64},{128,160},{160,128},{192,224},{224,1... | collective-permute-start | bytes 3538952 | tf_op jit(solution)/shard_map/ppermute | solution.py:30
  80.1 14.5 %collective-permute-start.14 = (f32[96,512]{1,0:T(8,128)S(1)}, f32[96,512]{1,0:T(8,128)S(1)}, u32[]{:S(2)}, u32[]{:S(2)}) collective-permute-start(f32[96,512]{1,0:T(8,128)S(1)} %bitcast.157), channel_id=1, source_target_pairs={{0,0},{1,32},{2,64},{3,96},{4,128},{5,160},{6,192},{7,224},{8,8},{... | collective-permute-start | bytes 589832 | tf_op jit(solution)/shard_map/ppermute | solution.py:50
  94.6 0.7 copy-start.7
  101.7 1.4 copy-start.2
  243.0 85.2 %copy-start = (f32[768,768]{1,0:T(8,128)S(1)}, f32[768,768]{1,0:T(8,128)}, u32[]{:S(2)}) copy-start(f32[768,768]{1,0:T(8,128)} %fusion.23) | copy-start | bytes 7077892
  347.4 1.6 copy-start.1
  352.8 4.4 %copy-start.3 = (f32[256,768]{1,0:T(8,128)S(1)}, f32[256,768]{1,0:T(8,128)}, u32[]{:S(2)}) copy-start(f32[256,768]{1,0:T(8,128)} %copy.23) | copy-start | bytes 2359300
Sparse Core Ops, SparseCore 0:
  95.5 82.3 all-gather.2

commit v2 on v1

v2 whole, which is shorter than its diff:
```python
import functools

import jax
import jax.numpy as jnp
from jax import lax
from jax.experimental import pallas as pl
from jax.experimental.pallas import tpu as pltpu
from jax.sharding import PartitionSpec as P

NB = 256
PANELS = 3
K = PANELS * NB
NY, NX, NZ = 4, 4, 8
HI = lax.Precision.HIGHEST
F32 = jnp.float32
BASE = 128
GROUP = 8


def dot(a, b, over):
    return lax.dot_general(a, b, (over, ((), ())), precision=HI, preferred_element_type=F32)


ROWS = ((1,), (0,))
TURN = ((0,), (0,))


def total(terms):
    while len(terms) > 1:
        terms = [terms[i] + terms[i + 1] if i + 1 < len(terms) else terms[i] for i in range(0, len(terms), 2)]
    return terms[0]


def factor_base(block, tasks):
    count = BASE // GROUP
    sub = lax.broadcasted_iota(jnp.int32, (GROUP, BASE), 0)
    lane = lax.broadcasted_iota(jnp.int32, (GROUP, BASE), 1)
    rows = [block[GROUP * h : GROUP * h + GROUP, :] for h in range(count)]

    def spread_row(a, i):
        return jnp.broadcast_to(a[i : i + 1, :], (GROUP, BASE))

    def spread_lane(a, j):
        return jnp.broadcast_to(a[:, j : j + 1], (GROUP, BASE))

    upper, inverse = [], []
    each = -(-len(tasks) // (count - 1))
    for g in range(count):
        lo, hi = GROUP * g, GROUP * g + GROUP
        inside = (lane >= lo) & (lane < hi)
        old = rows[g]
        pivot = [spread_lane(old, lo + j) for j in range(GROUP)]
        v = jnp.where(inside, jnp.where(lane == sub + lo, 1.0, 0.0), old)
        x = jnp.zeros((GROUP, BASE), F32)
        diag = jnp.ones((GROUP, BASE), F32)
        for i in range(GROUP):
            here = sub == i
            d = spread_row(pivot[i], i)
            scale = jnp.where(here, 0.0, pivot[i]) / d
            b = spread_row(v, i)
            x = jnp.where(here, b, x)
            diag = jnp.where(here, d, diag)
            for j in range(i + 1, GROUP):
                pivot[j] = pivot[j] - scale * spread_row(pivot[j], i)
            v = v - scale * b
        z = v / diag
        zs = [spread_row(z, k) for k in range(GROUP)]
        for h in range(g + 1, count):
            terms = [spread_lane(rows[h], lo + k) * zs[k] for k in range(GROUP)]
            rows[h] = jnp.where(inside, 0.0, rows[h]) - total(terms)
        x = x * lax.rsqrt(diag)
        corner = total([spread_lane(x, lo + k) * spread_row(old, k) for k in range(GROUP)])
        upper.append(jnp.where(lane >= hi, x, jnp.where(lane >= lo, corner, 0.0)))
        inverse.append(jnp.where(lane < hi, x, 0.0))
        for _ in range(each):
            if tasks:
                tasks.pop(0)()
    while tasks:
        tasks.pop(0)()
    return jnp.concatenate(upper, 0), jnp.concatenate(inverse, 0)


def factor_all(lt, inv, u, w, col):
    inv[...] = jnp.zeros((K, K), F32)
    w[...] = jnp.zeros((K, 2 * NB), F32)
    in_panel = col < PANELS
    block = lt[:BASE, :BASE]
    tasks = []
    for o in range(0, K, BASE):
        e = o + BASE
        xs, xi = factor_base(block, tasks)
        lt[o:e, o:e] = xs
        inv[o:e, o:e] = xi
        if e < K:
            n = e + BASE
            near = dot(xi, lt[o:e, e:n], ROWS)
            block = lt[e:n, e:n] - dot(near, near, TURN)
            lt[o:e, e:n] = near

        def panel(o=o, e=e, xi=xi):
            if e + BASE < K:
                lt[o:e, e + BASE :] = dot(xi, lt[o:e, e + BASE :], ROWS)

        def solve(o=o, e=e, xi=xi):
            u[o:e, :] = dot(xi, u[o:e, :], ROWS)

        def invert(o=o, e=e, xi=xi):
            if o:
                inv[o:e, :o] = dot(xi, inv[o:e, :o], ROWS)

        def weigh(o=o, e=e):
            sub = lax.broadcasted_iota(jnp.int32, (BASE, NB), 0)
            lane = lax.broadcasted_iota(jnp.int32, (BASE, NB), 1)
            unit = jnp.where(sub + o == lane + col * NB, -1.0, 0.0).astype(F32)
            left = jnp.where(in_panel, unit, u[o:e, :NB])
            right = u[o:e, NB:]
            for c in range(0, e, NB):
                t = min(c + NB, e)
                w[c:t, :NB] = w[c:t, :NB] + dot(inv[o:e, c:t], left, TURN)
                w[c:t, NB:] = w[c:t, NB:] + dot(inv[o:e, c:t], right, TURN)

        def trail(b, o=o, e=e):
            t = b + BASE
            p = lt[o:e, b:t]
            if b > e:
                lt[b:t, b:] = lt[b:t, b:] - dot(p, lt[o:e, b:], TURN)
            elif t < K:
                lt[b:t, t:] = lt[b:t, t:] - dot(p, lt[o:e, t:], TURN)

        def trail_inv(b, o=o, e=e):
            inv[b : b + BASE, :e] = inv[b : b + BASE, :e] - dot(lt[o:e, b : b + BASE], inv[o:e, :e], TURN)

        def trail_u(b, o=o, e=e):
            u[b : b + BASE, :] = u[b : b + BASE, :] - dot(lt[o:e, b : b + BASE], u[o:e, :], TURN)

        later = range(e, K, BASE)
        tasks = [panel] + [functools.partial(trail, b) for b in later] + [invert, solve]
        tasks += [functools.partial(trail_inv, b) for b in later]
        tasks += [functools.partial(trail_u, b) for b in later] + [weigh]
    while tasks:
        tasks.pop(0)()


def factor_kernel(at_ref, da_ref, db_ref, weights_ref, tile_ref, lt, inv, u, w, split, tile, sem):
    row, col = at_ref[0], at_ref[1]
    y_index, core = row // 2, row % 2
    for s in range(NY):
        y_from = (y_index + NY - s) % NY
        for d_from, which in ((da_ref, core), (db_ref, 1 - core)):
            at = 32 * (2 * y_from + which)
            lane = 0
            for p in range(PANELS):
                place = pl.ds(pl.multiple_of(p * NB + at, 32), 32)
                wide = K - p * NB
                lt[place, p * NB :] = d_from[s, :, lane : lane + wide]
                lane += wide
            for p in range(PANELS):
                place = pl.ds(pl.multiple_of(p * NB + at, 32), 32)
                u[place, :] = d_from[s, :, lane : lane + 2 * NB]
                lane += 2 * NB
    factor_all(lt, inv, u, w, col)

    for j in range(PANELS):
        o, e = j * NB, (j + 1) * NB
        hi = w[o:e, :].astype(jnp.bfloat16)
        lo = (w[o:e, :] - hi.astype(F32)).astype(jnp.bfloat16)
        for r in range(8):
            to, frm = r * 96 + j * 32, r * 32
            split[to : to + 32, : 2 * NB] = hi[frm : frm + 32, :]
            split[to : to + 32, 2 * NB :] = lo[frm : frm + 32, :]
    send = pltpu.make_async_copy(split, weights_ref, sem.at[0])
    send.start()

    tile[...] = jnp.zeros((NB, NB), F32)

    @pl.when((col < PANELS) & (row < PANELS) & (row >= col))
    def _():
        p_row = pl.multiple_of(row * NB, NB)
        p_col = pl.multiple_of(col * NB, NB)
        part = lt[pl.ds(p_col, NB), pl.ds(p_row, NB)]
        sub = lax.broadcasted_iota(jnp.int32, (NB, NB), 0)
        lane = lax.broadcasted_iota(jnp.int32, (NB, NB), 1)
        tile[...] = jnp.where((row > col) | (lane >= sub), part, 0.0).T

    send_tile = pltpu.make_async_copy(tile, tile_ref, sem.at[1])
    send_tile.start()
    send.wait()
    send_tile.wait()


def factor(place, da, db):
    vmem = pl.BlockSpec(memory_space=pltpu.VMEM)
    hbm = pl.BlockSpec(memory_space=pltpu.HBM)
    return pl.pallas_call(
        factor_kernel,
        in_specs=[pl.BlockSpec(memory_space=pltpu.SMEM), vmem, vmem],
        out_specs=[hbm, hbm],
        out_shape=[
            jax.ShapeDtypeStruct((K, 4 * NB), jnp.bfloat16),
            jax.ShapeDtypeStruct((NB, NB), F32),
        ],
        scratch_shapes=[
            pltpu.VMEM((K, K), F32),
            pltpu.VMEM((K, K), F32),
            pltpu.VMEM((K, 2 * NB), F32),
            pltpu.VMEM((K, 2 * NB), F32),
            pltpu.VMEM((K, 4 * NB), jnp.bfloat16),
            pltpu.VMEM((NB, NB), F32),
            pltpu.SemaphoreType.DMA((2,)),
        ],
        compiler_params=pltpu.CompilerParams(vmem_limit_bytes=28 * 2**20),
        cost_estimate=pl.CostEstimate(flops=4 * 10**9, bytes_accessed=10**7, transcendentals=0),
        name="factor",
    )(place, da, db)


def update_kernel(
    at_ref, weights_ref, tile_ref, cov_ref, rows_ref, out_ref, split, tile, buf, acc, own_sem, in_sem, cov_sem, out_sem
):
    row, col = at_ref[0], at_ref[1]

    def load(g):
        return pltpu.make_async_copy(rows_ref.at[g], buf.at[g], in_sem.at[g])

    def base(k):
        return pltpu.make_async_copy(cov_ref.at[k], acc.at[k], cov_sem.at[k])

    def store(k):
        return pltpu.make_async_copy(acc.at[k], out_ref.at[k], out_sem.at[k])

    get_weights = pltpu.make_async_copy(weights_ref, split, own_sem.at[0])
    get_tile = pltpu.make_async_copy(tile_ref, tile, own_sem.at[1])
    load(0).start()
    get_weights.start()
    get_tile.start()
    for g in range(4):
        if g:
            load(g).start()
        base(g).start()
        base(g + 4).start()
    get_weights.wait()
    get_tile.wait()

    def step(g, carry):
        load(g).wait()
        base(g).wait()
        base(g + 4).wait()
        over = (TURN, ((), ()))
        for l in range(2):
            k = l * 4 + g
            rows = buf[g, :, l * NB : (l + 1) * NB]
            hi = rows.astype(jnp.bfloat16)
            lo = (rows - hi.astype(F32)).astype(jnp.bfloat16)
            both = lax.dot_general(hi, split[...], over, preferred_element_type=F32)
            small = lax.dot_general(lo, split[:, : 2 * NB], over, preferred_element_type=F32)
            product = both[:, : 2 * NB] + (both[:, 2 * NB :] + small)
            for q in range(4):
                place = pl.ds(q, NB, stride=4)
                at = (q % 2) * NB + (q // 2) * 128
                left = acc[k, place, :]
                if q % 2 == 0:
                    left = jnp.where(col < PANELS, 0.0, left)
                acc[k, place, :] = left - product[:, at : at + 128]

        @pl.when((g == 0) & (row < PANELS))
        def _():
            for part in range(2):
                acc[0, pl.ds(2 * part, NB, stride=4), :] = tile[:, part * 128 : part * 128 + 128]
                acc[0, pl.ds(2 * part + 1, NB, stride=4), :] = jnp.zeros((NB, 128), F32)

        store(g).start()
        store(g + 4).start()
        return carry

    lax.fori_loop(0, 4, step, 0)
    for k in range(8):
        store(k).wait()


def update(place, weights, tile, cov, rows_t):
    hbm = pl.BlockSpec(memory_space=pltpu.HBM)
    return pl.pallas_call(
        update_kernel,
        in_specs=[pl.BlockSpec(memory_space=pltpu.SMEM)] + [hbm] * 4,
        out_specs=hbm,
        out_shape=jax.ShapeDtypeStruct((8, 4 * NB, 128), F32),
        scratch_shapes=[
            pltpu.VMEM((K, 4 * NB), jnp.bfloat16),
            pltpu.VMEM((NB, NB), F32),
            pltpu.VMEM((4, K, 2 * NB), F32),
            pltpu.VMEM((8, 4 * NB, 128), F32),
            pltpu.SemaphoreType.DMA((2,)),
            pltpu.SemaphoreType.DMA((4,)),
            pltpu.SemaphoreType.DMA((8,)),
            pltpu.SemaphoreType.DMA((8,)),
        ],
        compiler_params=pltpu.CompilerParams(vmem_limit_bytes=60 * 2**20),
        cost_estimate=pl.CostEstimate(flops=5 * 10**9, bytes_accessed=16 * 10**6, transcendentals=0),
        name="update",
    )(place, weights, tile, cov, rows_t)


def row_perm(shift):
    return [(y * 2 + core, ((y + shift) % NY) * 2 + core) for y in range(NY) for core in range(2)]


def x_perm(shift, limit):
    return [(z * NX + x, z * NX + (x + shift) % NX) for z in range(NZ) for x in range(limit)]


def z_perm(step):
    pairs = [(z, z + step) for z in range(0, NZ, 2 * step)]
    return [(a * NX + x, b * NX + x) for a, b in pairs for x in range(PANELS)]


CORES = [(2 * y + core, 2 * y + 1 - core) for y in range(NY) for core in range(2)]


def after(arrays, *done):
    return lax.optimization_barrier((tuple(arrays), done))[0]


def gather_row(block):
    return [block] + [lax.ppermute(block, "row", row_perm(s)) for s in (1, 2, 3)]


def turn_pairs():
    return [(q * 32 + g * 8 + m, m * 32 + g * 8 + q) for q in range(8) for g in range(4) for m in range(8)]


def shards(covariance):
    row = lax.axis_index("row")
    col = lax.axis_index("col")
    place = jnp.stack([row, col]).astype(jnp.int32)
    z_index, x_index = col // NX, col % NX
    top = covariance[0].reshape(NB, 2 * NB)
    cov = covariance.reshape(8, NB, 2, 2, 128).transpose(0, 1, 3, 2, 4).reshape(8, 4 * NB, 128)
    piece = lax.all_to_all(top, "row", 0, 0, tiled=True)[: K // 8]

    turned = lax.ppermute(piece, ("row", "col"), turn_pairs())
    (part,) = after((piece[:, :NB],), place)
    for step in (4, 2, 1):
        got = lax.ppermute(part, "col", z_perm(step))
        part = jnp.where(z_index % (2 * step) == step, got, part)
        if step == 4:
            (turned,) = after((turned,), part)
    rows_t = lax.all_gather(turned, "col", axis=0).reshape(4, K, 2 * NB)

    around = [part] + [lax.ppermute(part, "col", x_perm(s, PANELS)) for s in (1, 2, 3)]
    wide = []
    for q in range(PANELS):
        s = (x_index + NX - q) % NX
        pick = jnp.where(s < 2, jnp.where(s == 0, around[0], around[1]), jnp.where(s == 2, around[2], around[3]))
        wide.append(pick)
    wide = [wide[q][32 * p : 32 * p + 32] for p in range(PANELS) for q in range(p, PANELS)]
    wide = jnp.concatenate(wide + [piece[32 * p : 32 * p + 32] for p in range(PANELS)], axis=1)
    da = jnp.stack(gather_row(wide))
    db = lax.ppermute(da, "row", CORES)

    weights, tile = factor(place, da, db)
    out = update(place, weights, tile, cov, rows_t)
    return out.reshape(8, NB, 2, 2, 128).transpose(0, 1, 3, 2, 4).reshape(8, NB, 2, NB)


def solution(mesh):
    return jax.shard_map(
        shards,
        mesh=mesh,
        in_specs=(P(None, "row", None, "col"),),
        out_specs=P(None, "row", None, "col"),
        check_vma=False,
    )
```

time: 411 us -> 151 us (0.37)
  the two profiles are of different devices: /device:TPU:249 before, /device:TPU:1 now
where the time goes in v2:
time: 151 us; the launch traced here: 149 us
  Pallas kernels  47.5 us (31%)
  waiting for transfers between devices  43.8 us (29%)
  starting transfers between devices  38.9 us (26%)
  between operations  13.8 us (9%)
  local copies, waits for them, and re-layouts  5.08 us (3%)
    pallas_call x1, Pallas kernels, factor(): pl.pallas_call(factor_kernel, in_specs=[pl.BlockSpec(memory_space=pltpu.S...  35.7 us
    ppermute x3, waiting for transfers between devices, gather_row(): lax.ppermute(block, 'row', row_perm(s))  19.5 us
    ppermute x3, starting transfers between devices, shards(): lax.ppermute(part, 'col', x_perm(s, PANELS))  13.3 us
    pallas_call x1, Pallas kernels, update(): pl.pallas_call(update_kernel, in_specs=[pl.BlockSpec(memory_space=pltpu.S...  11.8 us
    ppermute x3, starting transfers between devices, shards(): got = lax.ppermute(part, 'col', z_perm(step))  11.2 us
    all_to_all x1, waiting for transfers between devices, shards(): piece = lax.all_to_all(top, 'row', 0, 0, tiled=True)[:K // 8]  9.42 us
    all_to_all x1, starting transfers between devices, shards(): piece = lax.all_to_all(top, 'row', 0, 0, tiled=True)[:K // 8]  6.64 us
    ppermute x1, waiting for transfers between devices, shards(): turned = lax.ppermute(piece, ('row', 'col'), turn_pairs())  4.91 us
  transfers between devices with their start and end apart: 13, of which 11 were waited for; matrix products, arithmetic and copies ran while one was open for 0% of the time, Pallas kernels for 24%

profile of v2, /device:TPU:1, one launch (start us, length us, event | category | flops | bytes accessed | tf_op | source)
XLA Modules:
  0.0 149.3 jit_solution(9625418400962139260)
XLA Ops:
  6.5 1.2 slice.52
  7.8 1.2 all_to_all.8
  9.0 6.6 %all-to-all-start = ((f32[8,32,512]{2,1,0:T(8,128)}), f32[8,32,512]{2,1,0:T(8,128)S(1)}, u32[]{:S(2)}, u32[]{:S(2)}) async-start(f32[8,32,512]{2,1,0:T(8,128)} %all_to_all.8), calls=%async_computation | async-start | bytes 1048576 | tf_op jit(solution)/shard_map/all_to_all | solution.py:338
  15.6 0.0 all-gather.3.cloned.1.call-start
  15.6 0.1 pad_add_fusion.at_ref
  15.7 0.0 copy-start
  15.7 9.4 %all-to-all-done = f32[8,32,512]{2,1,0:T(8,128)S(1)} async-done(((f32[8,32,512]{2,1,0:T(8,128)}), f32[8,32,512]{2,1,0:T(8,128)S(1)}, u32[]{:S(2)}, u32[]{:S(2)}) %all-to-all-start) | async-done | bytes 524320 | tf_op jit(solution)/shard_map/all_to_all | solution.py:338
  25.1 8.1 %collective-permute-start = (f32[96,256]{1,0:T(8,128)S(1)}, f32[96,256]{1,0:T(8,128)S(1)}, u32[]{:S(2)}, u32[]{:S(2)}) collective-permute-start(f32[96,256]{1,0:T(8,128)S(1)} %slice.68), channel_id=1, source_target_pairs={{0,16},{1,17},{2,18},{32,48},{33,49},{34,50},{64,80},{65,81},{66,8... | collective-permute-start | bytes 294920 | tf_op jit(solution)/shard_map/ppermute | solution.py:343
  33.3 4.2 %collective-permute-start.10 = (f32[96,512]{1,0:T(8,128)S(1)}, f32[96,512]{1,0:T(8,128)S(1)}, u32[]{:S(2)}, u32[]{:S(2)}) collective-permute-start(f32[96,512]{1,0:T(8,128)S(1)} %bitcast.36), channel_id=1, source_target_pairs={{0,0},{1,32},{2,64},{3,96},{4,128},{5,160},{6,192},{7,224},{8,8},{... | collective-permute-start | bytes 589832 | tf_op jit(solution)/shard_map/ppermute | solution.py:340
  37.5 0.0 collective-permute-done
  37.5 4.9 %collective-permute-done.10 = f32[96,512]{1,0:T(8,128)S(1)} collective-permute-done((f32[96,512]{1,0:T(8,128)S(1)}, f32[96,512]{1,0:T(8,128)S(1)}, u32[]{:S(2)}, u32[]{:S(2)}) %collective-permute-start.10) | collective-permute-done | bytes 196640 | tf_op jit(solution)/shard_map/ppermute | solution.py:340
  42.4 0.0 copy-start.3
  42.4 0.7 copy-done.3
  43.1 0.0 all-gather.3.cloned.1.call-update
  43.1 1.3 collective-permute-start.1
  44.5 1.6 %collective-permute-done.1 = f32[96,256]{1,0:T(8,128)S(1)} collective-permute-done((f32[96,256]{1,0:T(8,128)S(1)}, f32[96,256]{1,0:T(8,128)S(1)}, u32[]{:S(2)}, u32[]{:S(2)}) %collective-permute-start.1) | collective-permute-done | bytes 98336 | tf_op jit(solution)/shard_map/ppermute | solution.py:343
  46.1 1.8 %collective-permute-start.2 = (f32[96,256]{1,0:T(8,128)S(1)}, f32[96,256]{1,0:T(8,128)S(1)}, u32[]{:S(2)}, u32[]{:S(2)}) collective-permute-start(f32[96,256]{1,0:T(8,128)S(1)} %broadcast_select_fusion.1), channel_id=1, source_target_pairs={{0,4},{1,5},{2,6},{8,12},{9,13},{10,14},{16,20},{17,21},{18,22},{2... | collective-permute-start | bytes 294920 | tf_op jit(solution)/shard_map/ppermute | solution.py:343
  47.9 2.0 %collective-permute-done.2 = f32[96,256]{1,0:T(8,128)S(1)} collective-permute-done((f32[96,256]{1,0:T(8,128)S(1)}, f32[96,256]{1,0:T(8,128)S(1)}, u32[]{:S(2)}, u32[]{:S(2)}) %collective-permute-start.2) | collective-permute-done | bytes 98336 | tf_op jit(solution)/shard_map/ppermute | solution.py:343
  49.9 1.9 %collective-permute-start.5 = (f32[96,256]{1,0:T(8,128)S(1)}, f32[96,256]{1,0:T(8,128)S(1)}, u32[]{:S(2)}, u32[]{:S(2)}) collective-permute-start(f32[96,256]{1,0:T(8,128)S(1)} %broadcast_select_fusion.2), channel_id=1, source_target_pairs={{0,3},{1,0},{2,1},{4,7},{5,4},{6,5},{8,11},{9,8},{10,9},{12,15},{1... | collective-permute-start | bytes 294920 | tf_op jit(solution)/shard_map/ppermute | solution.py:349
  51.8 10.1 %collective-permute-start.4 = (f32[96,256]{1,0:T(8,128)S(1)}, f32[96,256]{1,0:T(8,128)S(1)}, u32[]{:S(2)}, u32[]{:S(2)}) collective-permute-start(f32[96,256]{1,0:T(8,128)S(1)} %broadcast_select_fusion.2), channel_id=1, source_target_pairs={{0,2},{1,3},{2,0},{4,6},{5,7},{6,4},{8,10},{9,11},{10,8},{12,14},{... | collective-permute-start | bytes 294920 | tf_op jit(solution)/shard_map/ppermute | solution.py:349
  61.9 1.3 collective-permute-start.3
  63.2 0.0 collective-permute-done.5
  63.3 0.8 collective-permute-done.4
  64.0 0.8 collective-permute-done.3
  65.0 1.4 collective-permute-start.8
  66.3 1.5 collective-permute-start.7
  67.8 0.0 collective-permute-start.6
  67.8 6.3 %collective-permute-done.8 = f32[32,3072]{1,0:T(8,128)S(1)} collective-permute-done((f32[32,3072]{1,0:T(8,128)S(1)}, f32[32,3072]{1,0:T(8,128)S(1)}, u32[]{:S(2)}, u32[]{:S(2)}) %collective-permute-start.8) | collective-permute-done | bytes 393248 | tf_op jit(solution)/shard_map/ppermute | solution.py:324
  74.2 2.2 %collective-permute-done.7 = f32[32,3072]{1,0:T(8,128)S(1)} collective-permute-done((f32[32,3072]{1,0:T(8,128)S(1)}, f32[32,3072]{1,0:T(8,128)S(1)}, u32[]{:S(2)}, u32[]{:S(2)}) %collective-permute-start.7) | collective-permute-done | bytes 393248 | tf_op jit(solution)/shard_map/ppermute | solution.py:324
  76.3 11.0 %collective-permute-done.6 = f32[32,3072]{1,0:T(8,128)S(1)} collective-permute-done((f32[32,3072]{1,0:T(8,128)S(1)}, f32[32,3072]{1,0:T(8,128)S(1)}, u32[]{:S(2)}, u32[]{:S(2)}) %collective-permute-start.6) | collective-permute-done | bytes 393248 | tf_op jit(solution)/shard_map/ppermute | solution.py:324
  87.3 0.1 pad_maximum_fusion.da_ref
  87.4 0.8 collective-permute-start.9
  88.2 3.0 %collective-permute-done.9.db_ref = f32[4,32,3072]{2,1,0:T(8,128)S(1)} collective-permute-done((f32[4,32,3072]{2,1,0:T(8,128)S(1)}, f32[4,32,3072]{2,1,0:T(8,128)S(1)}, u32[]{:S(2)}, u32[]{:S(2)}) %collective-permute-start.9) | collective-permute-done | bytes 1572896 | tf_op jit(solution)/shard_map/ppermute | solution.py:358
  91.2 0.0 copy-done
  91.2 35.7 %factor.1 = (bf16[768,1024]{1,0:T(8,128)(2,1)S(1)}, f32[256,256]{1,0:T(8,128)S(1)}) custom-call(s32[2]{0:T(128)S(1)} %pad_add_fusion.at_ref, f32[4,32,3072]{2,1,0:T(8,128)S(1)} %pad_maximum_fusion.da_ref, f32[4,32,3072]{2,1,0:T(8,128)S(1)} %collective-permute-done.9.db_ref), custom_call_target="tpu_custom_call" | custom-call | flops 4000000000 | bytes 10000000 | tf_op jit(solution)/shard_map/factor/pallas_call | solution.py:194
  126.9 0.0 copy-start.1
  126.9 1.1 copy-done.1
  128.0 0.0 copy-start.2
  128.0 0.8 copy-done.2
  128.8 1.8 %all-gather.3.cloned.1.call-done = f32[3072,512]{1,0:T(8,128)} async-done(((f32[96,512]{1,0:T(8,128)}), f32[3072,512]{1,0:T(8,128)}) %all-gather.3.cloned.1.call-update) | async-done | bytes 6291472 | tf_op jit(solution)/shard_map/all_gather | solution.py:347
  130.6 11.8 %update.1 = f32[8,1024,128]{2,1,0:T(8,128)} custom-call(s32[2]{0:T(128)} %copy-done, bf16[768,1024]{1,0:T(8,128)(2,1)} %copy-done.1, f32[256,256]{1,0:T(8,128)} %copy-done.2, f32[8,1024,128]{2,1,0:T(8,128)} %bitcast.37, f32[4,768,512]{2,1,0:T(8,128)} %bitcast.38), custom_call_target="tpu_custom_call" | custom-call | flops 5000000000 | bytes 16000000 | tf_op jit(solution)/shard_map/update/pallas_call | solution.py:282
  (15 shorter events, 0.1 us)
Async XLA Ops:
  9.0 16.1 %all-to-all-start = ((f32[8,32,512]{2,1,0:T(8,128)}), f32[8,32,512]{2,1,0:T(8,128)S(1)}, u32[]{:S(2)}, u32[]{:S(2)}) async-start(f32[8,32,512]{2,1,0:T(8,128)} %all_to_all.8), calls=%async_computation | async-start | bytes 1048576 | tf_op jit(solution)/shard_map/all_to_all | solution.py:338
  15.6 115.0 %all-gather.3.cloned.1.call-start = ((), (), s32[]{:S(2)}) async-start(), calls=%async_computation.1 | async-start | bytes 6488064 | tf_op jit(solution)/shard_map/all_gather | solution.py:347
  15.7 75.5 %copy-start = (s32[2]{0:T(128)}, s32[2]{0:T(128)S(1)}, u32[]{:S(2)}) copy-start(s32[2]{0:T(128)S(1)} %pad_add_fusion.at_ref) | copy-start | bytes 28
  25.1 12.4 %collective-permute-start = (f32[96,256]{1,0:T(8,128)S(1)}, f32[96,256]{1,0:T(8,128)S(1)}, u32[]{:S(2)}, u32[]{:S(2)}) collective-permute-start(f32[96,256]{1,0:T(8,128)S(1)} %slice.68), channel_id=1, source_target_pairs={{0,16},{1,17},{2,18},{32,48},{33,49},{34,50},{64,80},{65,81},{66,8... | collective-permute-start | bytes 294920 | tf_op jit(solution)/shard_map/ppermute | solution.py:343
  33.3 9.1 %collective-permute-start.10 = (f32[96,512]{1,0:T(8,128)S(1)}, f32[96,512]{1,0:T(8,128)S(1)}, u32[]{:S(2)}, u32[]{:S(2)}) collective-permute-start(f32[96,512]{1,0:T(8,128)S(1)} %bitcast.36), channel_id=1, source_target_pairs={{0,0},{1,32},{2,64},{3,96},{4,128},{5,160},{6,192},{7,224},{8,8},{... | collective-permute-start | bytes 589832 | tf_op jit(solution)/shard_map/ppermute | solution.py:340
  42.4 0.7 copy-start.3
  43.1 2.9 %collective-permute-start.1 = (f32[96,256]{1,0:T(8,128)S(1)}, f32[96,256]{1,0:T(8,128)S(1)}, u32[]{:S(2)}, u32[]{:S(2)}) collective-permute-start(f32[96,256]{1,0:T(8,128)S(1)} %broadcast_select_fusion), channel_id=1, source_target_pairs={{0,8},{1,9},{2,10},{16,24},{17,25},{18,26},{32,40},{33,41},{34,42}... | collective-permute-start | bytes 294920 | tf_op jit(solution)/shard_map/ppermute | solution.py:343
  46.1 3.8 %collective-permute-start.2 = (f32[96,256]{1,0:T(8,128)S(1)}, f32[96,256]{1,0:T(8,128)S(1)}, u32[]{:S(2)}, u32[]{:S(2)}) collective-permute-start(f32[96,256]{1,0:T(8,128)S(1)} %broadcast_select_fusion.1), channel_id=1, source_target_pairs={{0,4},{1,5},{2,6},{8,12},{9,13},{10,14},{16,20},{17,21},{18,22},{2... | collective-permute-start | bytes 294920 | tf_op jit(solution)/shard_map/ppermute | solution.py:343
  49.9 13.4 %collective-permute-start.5 = (f32[96,256]{1,0:T(8,128)S(1)}, f32[96,256]{1,0:T(8,128)S(1)}, u32[]{:S(2)}, u32[]{:S(2)}) collective-permute-start(f32[96,256]{1,0:T(8,128)S(1)} %broadcast_select_fusion.2), channel_id=1, source_target_pairs={{0,3},{1,0},{2,1},{4,7},{5,4},{6,5},{8,11},{9,8},{10,9},{12,15},{1... | collective-permute-start | bytes 294920 | tf_op jit(solution)/shard_map/ppermute | solution.py:349
  51.8 12.2 %collective-permute-start.4 = (f32[96,256]{1,0:T(8,128)S(1)}, f32[96,256]{1,0:T(8,128)S(1)}, u32[]{:S(2)}, u32[]{:S(2)}) collective-permute-start(f32[96,256]{1,0:T(8,128)S(1)} %broadcast_select_fusion.2), channel_id=1, source_target_pairs={{0,2},{1,3},{2,0},{4,6},{5,7},{6,4},{8,10},{9,11},{10,8},{12,14},{... | collective-permute-start | bytes 294920 | tf_op jit(solution)/shard_map/ppermute | solution.py:349
  61.9 2.9 %collective-permute-start.3 = (f32[96,256]{1,0:T(8,128)S(1)}, f32[96,256]{1,0:T(8,128)S(1)}, u32[]{:S(2)}, u32[]{:S(2)}) collective-permute-start(f32[96,256]{1,0:T(8,128)S(1)} %broadcast_select_fusion.2), channel_id=1, source_target_pairs={{0,1},{1,2},{2,3},{4,5},{5,6},{6,7},{8,9},{9,10},{10,11},{12,13},{... | collective-permute-start | bytes 294920 | tf_op jit(solution)/shard_map/ppermute | solution.py:349
  65.0 9.2 %collective-permute-start.8 = (f32[32,3072]{1,0:T(8,128)S(1)}, f32[32,3072]{1,0:T(8,128)S(1)}, u32[]{:S(2)}, u32[]{:S(2)}) collective-permute-start(f32[32,3072]{1,0:T(8,128)S(1)} %fusion), channel_id=1, source_target_pairs={{0,192},{32,224},{64,0},{96,32},{128,64},{160,96},{192,128},{224,1... | collective-permute-start | bytes 1179656 | tf_op jit(solution)/shard_map/ppermute | solution.py:324
  66.3 10.0 %collective-permute-start.7 = (f32[32,3072]{1,0:T(8,128)S(1)}, f32[32,3072]{1,0:T(8,128)S(1)}, u32[]{:S(2)}, u32[]{:S(2)}) collective-permute-start(f32[32,3072]{1,0:T(8,128)S(1)} %fusion), channel_id=1, source_target_pairs={{0,128},{32,160},{64,192},{96,224},{128,0},{160,32},{192,64},{224,... | collective-permute-start | bytes 1179656 | tf_op jit(solution)/shard_map/ppermute | solution.py:324
  67.8 19.5 %collective-permute-start.6 = (f32[32,3072]{1,0:T(8,128)S(1)}, f32[32,3072]{1,0:T(8,128)S(1)}, u32[]{:S(2)}, u32[]{:S(2)}) collective-permute-start(f32[32,3072]{1,0:T(8,128)S(1)} %fusion), channel_id=1, source_target_pairs={{0,64},{32,96},{64,128},{96,160},{128,192},{160,224},{192,0},{224,... | collective-permute-start | bytes 1179656 | tf_op jit(solution)/shard_map/ppermute | solution.py:324
  87.4 3.8 %collective-permute-start.9 = (f32[4,32,3072]{2,1,0:T(8,128)S(1)}, f32[4,32,3072]{2,1,0:T(8,128)S(1)}, u32[]{:S(2)}, u32[]{:S(2)}) collective-permute-start(f32[4,32,3072]{2,1,0:T(8,128)S(1)} %pad_maximum_fusion.da_ref), channel_id=1, source_target_pairs={{0,32},{32,0},{64,96},{96,64},{128,160},{160,128},{192,224},{224,1... | collective-permute-start | bytes 4718600 | tf_op jit(solution)/shard_map/ppermute | solution.py:358
  126.9 1.1 copy-start.1
  128.0 0.8 copy-start.2
Sparse Core Ops, SparseCore 0:
  43.3 87.2 all-gather.2

commit v3 on v2

--- a/solution.py
+++ b/solution.py
@@ -141,7 +141,7 @@
         tasks.pop(0)()
 
 
-def factor_kernel(at_ref, da_ref, db_ref, weights_ref, tile_ref, lt, inv, u, w, split, tile, sem):
+def factor_kernel(at_ref, da_ref, db_ref, split, tile, lt, inv, u, w):
     row, col = at_ref[0], at_ref[1]
     y_index, core = row // 2, row % 2
     for s in range(NY):
@@ -165,12 +165,9 @@
         hi = w[o:e, :].astype(jnp.bfloat16)
         lo = (w[o:e, :] - hi.astype(F32)).astype(jnp.bfloat16)
         for r in range(8):
-            to, frm = r * 96 + j * 32, r * 32
-            split[to : to + 32, : 2 * NB] = hi[frm : frm + 32, :]
-            split[to : to + 32, 2 * NB :] = lo[frm : frm + 32, :]
-    send = pltpu.make_async_copy(split, weights_ref, sem.at[0])
-    send.start()
-
+            to = pl.ds(pl.multiple_of((r ^ row) * 96 + j * 32, 32), 32)
+            split[to, : 2 * NB] = hi[r * 32 : r * 32 + 32, :]
+            split[to, 2 * NB :] = lo[r * 32 : r * 32 + 32, :]
     tile[...] = jnp.zeros((NB, NB), F32)
 
     @pl.when((col < PANELS) & (row < PANELS) & (row >= col))
@@ -182,19 +179,13 @@
         lane = lax.broadcasted_iota(jnp.int32, (NB, NB), 1)
         tile[...] = jnp.where((row > col) | (lane >= sub), part, 0.0).T
 
-    send_tile = pltpu.make_async_copy(tile, tile_ref, sem.at[1])
-    send_tile.start()
-    send.wait()
-    send_tile.wait()
-
 
 def factor(place, da, db):
     vmem = pl.BlockSpec(memory_space=pltpu.VMEM)
-    hbm = pl.BlockSpec(memory_space=pltpu.HBM)
     return pl.pallas_call(
         factor_kernel,
         in_specs=[pl.BlockSpec(memory_space=pltpu.SMEM), vmem, vmem],
-        out_specs=[hbm, hbm],
+        out_specs=[vmem] * 2,
         out_shape=[
             jax.ShapeDtypeStruct((K, 4 * NB), jnp.bfloat16),
             jax.ShapeDtypeStruct((NB, NB), F32),
@@ -204,9 +195,6 @@
             pltpu.VMEM((K, K), F32),
             pltpu.VMEM((K, 2 * NB), F32),
             pltpu.VMEM((K, 2 * NB), F32),
-            pltpu.VMEM((K, 4 * NB), jnp.bfloat16),
-            pltpu.VMEM((NB, NB), F32),
-            pltpu.SemaphoreType.DMA((2,)),
         ],
         compiler_params=pltpu.CompilerParams(vmem_limit_bytes=28 * 2**20),
         cost_estimate=pl.CostEstimate(flops=4 * 10**9, bytes_accessed=10**7, transcendentals=0),
@@ -214,9 +202,7 @@
     )(place, da, db)
 
 
-def update_kernel(
-    at_ref, weights_ref, tile_ref, cov_ref, rows_ref, out_ref, split, tile, buf, acc, own_sem, in_sem, cov_sem, out_sem
-):
+def update_kernel(at_ref, split, tile, cov_ref, rows_ref, out_ref, buf, acc, in_sem, cov_sem, out_sem):
     row, col = at_ref[0], at_ref[1]
 
     def load(g):
@@ -228,23 +214,22 @@
     def store(k):
         return pltpu.make_async_copy(acc.at[k], out_ref.at[k], out_sem.at[k])
 
-    get_weights = pltpu.make_async_copy(weights_ref, split, own_sem.at[0])
-    get_tile = pltpu.make_async_copy(tile_ref, tile, own_sem.at[1])
-    load(0).start()
-    get_weights.start()
-    get_tile.start()
-    for g in range(4):
-        if g:
-            load(g).start()
+    def fetch(g):
+        load(g).start()
         base(g).start()
         base(g + 4).start()
-    get_weights.wait()
-    get_tile.wait()
+
+    fetch(0)
 
     def step(g, carry):
         load(g).wait()
         base(g).wait()
         base(g + 4).wait()
+
+        @pl.when(g < 3)
+        def _():
+            fetch(g + 1)
+
         over = (TURN, ((), ()))
         for l in range(2):
             k = l * 4 + g
@@ -278,23 +263,21 @@
 
 
 def update(place, weights, tile, cov, rows_t):
+    vmem = pl.BlockSpec(memory_space=pltpu.VMEM)
     hbm = pl.BlockSpec(memory_space=pltpu.HBM)
     return pl.pallas_call(
         update_kernel,
-        in_specs=[pl.BlockSpec(memory_space=pltpu.SMEM)] + [hbm] * 4,
+        in_specs=[pl.BlockSpec(memory_space=pltpu.SMEM), vmem, vmem, hbm, hbm],
         out_specs=hbm,
         out_shape=jax.ShapeDtypeStruct((8, 4 * NB, 128), F32),
         scratch_shapes=[
-            pltpu.VMEM((K, 4 * NB), jnp.bfloat16),
-            pltpu.VMEM((NB, NB), F32),
             pltpu.VMEM((4, K, 2 * NB), F32),
             pltpu.VMEM((8, 4 * NB, 128), F32),
-            pltpu.SemaphoreType.DMA((2,)),
             pltpu.SemaphoreType.DMA((4,)),
             pltpu.SemaphoreType.DMA((8,)),
             pltpu.SemaphoreType.DMA((8,)),
         ],
-        compiler_params=pltpu.CompilerParams(vmem_limit_bytes=60 * 2**20),
+        compiler_params=pltpu.CompilerParams(vmem_limit_bytes=50 * 2**20),
         cost_estimate=pl.CostEstimate(flops=5 * 10**9, bytes_accessed=16 * 10**6, transcendentals=0),
         name="update",
     )(place, weights, tile, cov, rows_t)
@@ -325,7 +308,7 @@
 
 
 def turn_pairs():
-    return [(q * 32 + g * 8 + m, m * 32 + g * 8 + q) for q in range(8) for g in range(4) for m in range(8)]
+    return [(q * 32 + g * 8 + m, m * 32 + g * 8 + (q ^ m)) for q in range(8) for g in range(4) for m in range(8)]
 
 
 def shards(covariance):

time: 151 us -> 145 us (0.960); the launches traced: 149 us -> 145 us
  local copies, waits for them, and re-layouts: 5.08 us -> 3.18 us
  Pallas kernels: 47.5 us -> 45.6 us
  starting transfers between devices: 38.9 us -> 37.2 us
    ppermute x3, starting transfers between devices: 13.3 us -> 7.41 us  [shards(): lax.ppermute(part, 'col', x_perm(s, PANELS))]
    ppermute x3, starting transfers between devices: 2.88 us -> 6.1 us  [gather_row(): lax.ppermute(block, 'row', row_perm(s))]
    all_gather x1, waiting for transfers between devices: 1.79 us -> 4.52 us  [shards(): rows_t = lax.all_gather(turned, 'col', axis=0).reshape(4, K, 2 * NB)]
    ppermute x1, waiting for transfers between devices: 4.91 us -> 2.56 us  [shards(): turned = lax.ppermute(piece, ('row', 'col'), turn_pairs())]
    unnamed x15 -> x9, local copies, waits for them, and re-layouts: 2.61 us -> 0.72 us
    pallas_call x1, Pallas kernels: 11.8 us -> 10.1 us  [update(): pl.pallas_call(update_kernel, in_specs=[pl.BlockSpec(memory_space=pltpu.S...]
  transfers between devices with their start and end apart: 13 -> 13, of which waited for: 11 -> 9; matrix products, arithmetic and copies ran while one was open for 0% -> 0% of each run, Pallas kernels for 24% -> 25%
where the time goes in v3:
time: 145 us
  Pallas kernels  45.6 us (31%)
  waiting for transfers between devices  44.8 us (31%)
  starting transfers between devices  37.2 us (26%)
  between operations  13.7 us (9%)
  local copies, waits for them, and re-layouts  3.18 us (2%)
    pallas_call x1, Pallas kernels, factor(): pl.pallas_call(factor_kernel, in_specs=[pl.BlockSpec(memory_space=pltpu.S...  35.5 us
    ppermute x3, waiting for transfers between devices, gather_row(): lax.ppermute(block, 'row', row_perm(s))  19.6 us
    ppermute x3, starting transfers between devices, shards(): got = lax.ppermute(part, 'col', z_perm(step))  11.8 us
    pallas_call x1, Pallas kernels, update(): pl.pallas_call(update_kernel, in_specs=[pl.BlockSpec(memory_space=pltpu.S...  10.1 us
    all_to_all x1, waiting for transfers between devices, shards(): piece = lax.all_to_all(top, 'row', 0, 0, tiled=True)[:K // 8]  9.42 us
    ppermute x3, starting transfers between devices, shards(): lax.ppermute(part, 'col', x_perm(s, PANELS))  7.41 us
    all_to_all x1, starting transfers between devices, shards(): piece = lax.all_to_all(top, 'row', 0, 0, tiled=True)[:K // 8]  6.64 us
    ppermute x3, starting transfers between devices, gather_row(): lax.ppermute(block, 'row', row_perm(s))  6.1 us
  transfers between devices with their start and end apart: 13, of which 9 were waited for; matrix products, arithmetic and copies ran while one was open for 0% of the time, Pallas kernels for 25%

profile of v3, /device:TPU:1, one launch (start us, length us, event | category | flops | bytes accessed | tf_op | source)
XLA Modules:
  0.0 144.8 jit_solution(8520242028771556728)
XLA Ops:
  6.5 1.2 slice.52
  7.8 1.2 all_to_all.8
  9.0 6.6 %all-to-all-start = ((f32[8,32,512]{2,1,0:T(8,128)}), f32[8,32,512]{2,1,0:T(8,128)S(1)}, u32[]{:S(2)}, u32[]{:S(2)}) async-start(f32[8,32,512]{2,1,0:T(8,128)} %all_to_all.8), calls=%async_computation | async-start | bytes 1048576 | tf_op jit(solution)/shard_map/all_to_all | solution.py:321
  15.6 0.0 all-gather.3.cloned.1.call-start
  15.6 0.1 pad_add_fusion.at_ref
  15.7 9.4 %all-to-all-done = f32[8,32,512]{2,1,0:T(8,128)S(1)} async-done(((f32[8,32,512]{2,1,0:T(8,128)}), f32[8,32,512]{2,1,0:T(8,128)S(1)}, u32[]{:S(2)}, u32[]{:S(2)}) %all-to-all-start) | async-done | bytes 524320 | tf_op jit(solution)/shard_map/all_to_all | solution.py:321
  25.1 8.1 %collective-permute-start = (f32[96,256]{1,0:T(8,128)S(1)}, f32[96,256]{1,0:T(8,128)S(1)}, u32[]{:S(2)}, u32[]{:S(2)}) collective-permute-start(f32[96,256]{1,0:T(8,128)S(1)} %slice.68), channel_id=1, source_target_pairs={{0,16},{1,17},{2,18},{32,48},{33,49},{34,50},{64,80},{65,81},{66,8... | collective-permute-start | bytes 294920 | tf_op jit(solution)/shard_map/ppermute | solution.py:326
  33.3 4.2 %collective-permute-start.10 = (f32[96,512]{1,0:T(8,128)S(1)}, f32[96,512]{1,0:T(8,128)S(1)}, u32[]{:S(2)}, u32[]{:S(2)}) collective-permute-start(f32[96,512]{1,0:T(8,128)S(1)} %bitcast.36), channel_id=1, source_target_pairs={{0,0},{1,33},{2,66},{3,99},{4,132},{5,165},{6,198},{7,231},{8,8},{... | collective-permute-start | bytes 589832 | tf_op jit(solution)/shard_map/ppermute | solution.py:323
  37.5 0.0 collective-permute-done
  37.5 2.6 %collective-permute-done.10 = f32[96,512]{1,0:T(8,128)S(1)} collective-permute-done((f32[96,512]{1,0:T(8,128)S(1)}, f32[96,512]{1,0:T(8,128)S(1)}, u32[]{:S(2)}, u32[]{:S(2)}) %collective-permute-start.10) | collective-permute-done | bytes 196640 | tf_op jit(solution)/shard_map/ppermute | solution.py:323
  40.1 0.0 copy-start
  40.1 0.7 copy-done
  40.8 0.0 all-gather.3.cloned.1.call-update
  40.8 1.3 collective-permute-start.1
  42.1 1.6 %collective-permute-done.1 = f32[96,256]{1,0:T(8,128)S(1)} collective-permute-done((f32[96,256]{1,0:T(8,128)S(1)}, f32[96,256]{1,0:T(8,128)S(1)}, u32[]{:S(2)}, u32[]{:S(2)}) %collective-permute-start.1) | collective-permute-done | bytes 98336 | tf_op jit(solution)/shard_map/ppermute | solution.py:326
  43.7 2.4 %collective-permute-start.2 = (f32[96,256]{1,0:T(8,128)S(1)}, f32[96,256]{1,0:T(8,128)S(1)}, u32[]{:S(2)}, u32[]{:S(2)}) collective-permute-start(f32[96,256]{1,0:T(8,128)S(1)} %broadcast_select_fusion.1), channel_id=1, source_target_pairs={{0,4},{1,5},{2,6},{8,12},{9,13},{10,14},{16,20},{17,21},{18,22},{2... | collective-permute-start | bytes 294920 | tf_op jit(solution)/shard_map/ppermute | solution.py:326
  46.1 1.6 %collective-permute-done.2 = f32[96,256]{1,0:T(8,128)S(1)} collective-permute-done((f32[96,256]{1,0:T(8,128)S(1)}, f32[96,256]{1,0:T(8,128)S(1)}, u32[]{:S(2)}, u32[]{:S(2)}) %collective-permute-start.2) | collective-permute-done | bytes 98336 | tf_op jit(solution)/shard_map/ppermute | solution.py:326
  47.7 1.9 %collective-permute-start.5 = (f32[96,256]{1,0:T(8,128)S(1)}, f32[96,256]{1,0:T(8,128)S(1)}, u32[]{:S(2)}, u32[]{:S(2)}) collective-permute-start(f32[96,256]{1,0:T(8,128)S(1)} %broadcast_select_fusion.2), channel_id=1, source_target_pairs={{0,3},{1,0},{2,1},{4,7},{5,4},{6,5},{8,11},{9,8},{10,9},{12,15},{1... | collective-permute-start | bytes 294920 | tf_op jit(solution)/shard_map/ppermute | solution.py:332
  49.7 4.2 %collective-permute-start.4 = (f32[96,256]{1,0:T(8,128)S(1)}, f32[96,256]{1,0:T(8,128)S(1)}, u32[]{:S(2)}, u32[]{:S(2)}) collective-permute-start(f32[96,256]{1,0:T(8,128)S(1)} %broadcast_select_fusion.2), channel_id=1, source_target_pairs={{0,2},{1,3},{2,0},{4,6},{5,7},{6,4},{8,10},{9,11},{10,8},{12,14},{... | collective-permute-start | bytes 294920 | tf_op jit(solution)/shard_map/ppermute | solution.py:332
  53.9 1.3 collective-permute-start.3
  55.2 0.0 collective-permute-done.5
  55.2 2.4 %collective-permute-done.4 = f32[96,256]{1,0:T(8,128)S(1)} collective-permute-done((f32[96,256]{1,0:T(8,128)S(1)}, f32[96,256]{1,0:T(8,128)S(1)}, u32[]{:S(2)}, u32[]{:S(2)}) %collective-permute-start.4) | collective-permute-done | bytes 98336 | tf_op jit(solution)/shard_map/ppermute | solution.py:332
  57.6 0.0 collective-permute-done.3
  57.8 5.4 %collective-permute-start.8 = (f32[32,3072]{1,0:T(8,128)S(1)}, f32[32,3072]{1,0:T(8,128)S(1)}, u32[]{:S(2)}, u32[]{:S(2)}) collective-permute-start(f32[32,3072]{1,0:T(8,128)S(1)} %fusion), channel_id=1, source_target_pairs={{0,192},{32,224},{64,0},{96,32},{128,64},{160,96},{192,128},{224,1... | collective-permute-start | bytes 1179656 | tf_op jit(solution)/shard_map/ppermute | solution.py:307
  63.2 0.0 collective-permute-start.7
  63.2 0.7 collective-permute-start.6
  63.9 14.9 %collective-permute-done.8 = f32[32,3072]{1,0:T(8,128)S(1)} collective-permute-done((f32[32,3072]{1,0:T(8,128)S(1)}, f32[32,3072]{1,0:T(8,128)S(1)}, u32[]{:S(2)}, u32[]{:S(2)}) %collective-permute-start.8) | collective-permute-done | bytes 393248 | tf_op jit(solution)/shard_map/ppermute | solution.py:307
  78.7 0.0 collective-permute-done.7
  78.7 4.8 %collective-permute-done.6 = f32[32,3072]{1,0:T(8,128)S(1)} collective-permute-done((f32[32,3072]{1,0:T(8,128)S(1)}, f32[32,3072]{1,0:T(8,128)S(1)}, u32[]{:S(2)}, u32[]{:S(2)}) %collective-permute-start.6) | collective-permute-done | bytes 393248 | tf_op jit(solution)/shard_map/ppermute | solution.py:307
  83.5 0.1 pad_maximum_fusion.da_ref
  83.6 1.1 collective-permute-start.9
  84.7 3.0 %collective-permute-done.9.db_ref = f32[4,32,3072]{2,1,0:T(8,128)S(1)} collective-permute-done((f32[4,32,3072]{2,1,0:T(8,128)S(1)}, f32[4,32,3072]{2,1,0:T(8,128)S(1)}, u32[]{:S(2)}, u32[]{:S(2)}) %collective-permute-start.9) | collective-permute-done | bytes 1572896 | tf_op jit(solution)/shard_map/ppermute | solution.py:341
  87.8 35.5 %factor.1 = (bf16[768,1024]{1,0:T(8,128)(2,1)S(1)}, f32[256,256]{1,0:T(8,128)S(1)}) custom-call(s32[2]{0:T(128)S(1)} %pad_add_fusion.at_ref, f32[4,32,3072]{2,1,0:T(8,128)S(1)} %pad_maximum_fusion.da_ref, f32[4,32,3072]{2,1,0:T(8,128)S(1)} %collective-permute-done.9.db_ref), custom_call_target="tpu_custom_call" | custom-call | flops 4000000000 | bytes 10000000 | tf_op jit(solution)/shard_map/factor/pallas_call | solution.py:185
  123.3 4.5 %all-gather.3.cloned.1.call-done = f32[3072,512]{1,0:T(8,128)} async-done(((f32[96,512]{1,0:T(8,128)}), f32[3072,512]{1,0:T(8,128)}) %all-gather.3.cloned.1.call-update) | async-done | bytes 6291472 | tf_op jit(solution)/shard_map/all_gather | solution.py:330
  127.8 10.1 %update.1 = f32[8,1024,128]{2,1,0:T(8,128)} custom-call(s32[2]{0:T(128)S(1)} %pad_add_fusion.at_ref, bf16[768,1024]{1,0:T(8,128)(2,1)S(1)} %get-tuple-element.10.split, f32[256,256]{1,0:T(8,128)S(1)} %get-tuple-element.11.tile, f32[8,1024,128]{2,1,0:T(8,128)} %bitcast.37, f32[4,768,512]{2,1,0:T(8,128)} %bitcast.38), custom_call_target="tpu_custom_call" | custom-call | flops 5000000000 | bytes 16000000 | tf_op jit(solution)/shard_map/update/pallas_call | solution.py:268
  (15 shorter events, 0.1 us)
Async XLA Ops:
  9.0 16.1 %all-to-all-start = ((f32[8,32,512]{2,1,0:T(8,128)}), f32[8,32,512]{2,1,0:T(8,128)S(1)}, u32[]{:S(2)}, u32[]{:S(2)}) async-start(f32[8,32,512]{2,1,0:T(8,128)} %all_to_all.8), calls=%async_computation | async-start | bytes 1048576 | tf_op jit(solution)/shard_map/all_to_all | solution.py:321
  15.6 112.2 %all-gather.3.cloned.1.call-start = ((), (), s32[]{:S(2)}) async-start(), calls=%async_computation.1 | async-start | bytes 6488064 | tf_op jit(solution)/shard_map/all_gather | solution.py:330
  25.1 12.4 %collective-permute-start = (f32[96,256]{1,0:T(8,128)S(1)}, f32[96,256]{1,0:T(8,128)S(1)}, u32[]{:S(2)}, u32[]{:S(2)}) collective-permute-start(f32[96,256]{1,0:T(8,128)S(1)} %slice.68), channel_id=1, source_target_pairs={{0,16},{1,17},{2,18},{32,48},{33,49},{34,50},{64,80},{65,81},{66,8... | collective-permute-start | bytes 294920 | tf_op jit(solution)/shard_map/ppermute | solution.py:326
  33.3 6.8 %collective-permute-start.10 = (f32[96,512]{1,0:T(8,128)S(1)}, f32[96,512]{1,0:T(8,128)S(1)}, u32[]{:S(2)}, u32[]{:S(2)}) collective-permute-start(f32[96,512]{1,0:T(8,128)S(1)} %bitcast.36), channel_id=1, source_target_pairs={{0,0},{1,33},{2,66},{3,99},{4,132},{5,165},{6,198},{7,231},{8,8},{... | collective-permute-start | bytes 589832 | tf_op jit(solution)/shard_map/ppermute | solution.py:323
  40.1 0.7 copy-start
  40.8 2.9 %collective-permute-start.1 = (f32[96,256]{1,0:T(8,128)S(1)}, f32[96,256]{1,0:T(8,128)S(1)}, u32[]{:S(2)}, u32[]{:S(2)}) collective-permute-start(f32[96,256]{1,0:T(8,128)S(1)} %broadcast_select_fusion), channel_id=1, source_target_pairs={{0,8},{1,9},{2,10},{16,24},{17,25},{18,26},{32,40},{33,41},{34,42}... | collective-permute-start | bytes 294920 | tf_op jit(solution)/shard_map/ppermute | solution.py:326
  43.7 4.0 %collective-permute-start.2 = (f32[96,256]{1,0:T(8,128)S(1)}, f32[96,256]{1,0:T(8,128)S(1)}, u32[]{:S(2)}, u32[]{:S(2)}) collective-permute-start(f32[96,256]{1,0:T(8,128)S(1)} %broadcast_select_fusion.1), channel_id=1, source_target_pairs={{0,4},{1,5},{2,6},{8,12},{9,13},{10,14},{16,20},{17,21},{18,22},{2... | collective-permute-start | bytes 294920 | tf_op jit(solution)/shard_map/ppermute | solution.py:326
  47.7 7.5 %collective-permute-start.5 = (f32[96,256]{1,0:T(8,128)S(1)}, f32[96,256]{1,0:T(8,128)S(1)}, u32[]{:S(2)}, u32[]{:S(2)}) collective-permute-start(f32[96,256]{1,0:T(8,128)S(1)} %broadcast_select_fusion.2), channel_id=1, source_target_pairs={{0,3},{1,0},{2,1},{4,7},{5,4},{6,5},{8,11},{9,8},{10,9},{12,15},{1... | collective-permute-start | bytes 294920 | tf_op jit(solution)/shard_map/ppermute | solution.py:332
  49.7 7.9 %collective-permute-start.4 = (f32[96,256]{1,0:T(8,128)S(1)}, f32[96,256]{1,0:T(8,128)S(1)}, u32[]{:S(2)}, u32[]{:S(2)}) collective-permute-start(f32[96,256]{1,0:T(8,128)S(1)} %broadcast_select_fusion.2), channel_id=1, source_target_pairs={{0,2},{1,3},{2,0},{4,6},{5,7},{6,4},{8,10},{9,11},{10,8},{12,14},{... | collective-permute-start | bytes 294920 | tf_op jit(solution)/shard_map/ppermute | solution.py:332
  53.9 3.7 %collective-permute-start.3 = (f32[96,256]{1,0:T(8,128)S(1)}, f32[96,256]{1,0:T(8,128)S(1)}, u32[]{:S(2)}, u32[]{:S(2)}) collective-permute-start(f32[96,256]{1,0:T(8,128)S(1)} %broadcast_select_fusion.2), channel_id=1, source_target_pairs={{0,1},{1,2},{2,3},{4,5},{5,6},{6,7},{8,9},{9,10},{10,11},{12,13},{... | collective-permute-start | bytes 294920 | tf_op jit(solution)/shard_map/ppermute | solution.py:332
  57.8 21.0 %collective-permute-start.8 = (f32[32,3072]{1,0:T(8,128)S(1)}, f32[32,3072]{1,0:T(8,128)S(1)}, u32[]{:S(2)}, u32[]{:S(2)}) collective-permute-start(f32[32,3072]{1,0:T(8,128)S(1)} %fusion), channel_id=1, source_target_pairs={{0,192},{32,224},{64,0},{96,32},{128,64},{160,96},{192,128},{224,1... | collective-permute-start | bytes 1179656 | tf_op jit(solution)/shard_map/ppermute | solution.py:307
  63.2 15.5 %collective-permute-start.7 = (f32[32,3072]{1,0:T(8,128)S(1)}, f32[32,3072]{1,0:T(8,128)S(1)}, u32[]{:S(2)}, u32[]{:S(2)}) collective-permute-start(f32[32,3072]{1,0:T(8,128)S(1)} %fusion), channel_id=1, source_target_pairs={{0,128},{32,160},{64,192},{96,224},{128,0},{160,32},{192,64},{224,... | collective-permute-start | bytes 1179656 | tf_op jit(solution)/shard_map/ppermute | solution.py:307
  63.2 20.3 %collective-permute-start.6 = (f32[32,3072]{1,0:T(8,128)S(1)}, f32[32,3072]{1,0:T(8,128)S(1)}, u32[]{:S(2)}, u32[]{:S(2)}) collective-permute-start(f32[32,3072]{1,0:T(8,128)S(1)} %fusion), channel_id=1, source_target_pairs={{0,64},{32,96},{64,128},{96,160},{128,192},{160,224},{192,0},{224,... | collective-permute-start | bytes 1179656 | tf_op jit(solution)/shard_map/ppermute | solution.py:307
  83.6 4.2 %collective-permute-start.9 = (f32[4,32,3072]{2,1,0:T(8,128)S(1)}, f32[4,32,3072]{2,1,0:T(8,128)S(1)}, u32[]{:S(2)}, u32[]{:S(2)}) collective-permute-start(f32[4,32,3072]{2,1,0:T(8,128)S(1)} %pad_maximum_fusion.da_ref), channel_id=1, source_target_pairs={{0,32},{32,0},{64,96},{96,64},{128,160},{160,128},{192,224},{224,1... | collective-permute-start | bytes 4718600 | tf_op jit(solution)/shard_map/ppermute | solution.py:341
Sparse Core Ops, SparseCore 0:
  40.9 86.8 all-gather.2

commit v4 on v3

--- a/solution.py
+++ b/solution.py
@@ -205,8 +205,9 @@
 def update_kernel(at_ref, split, tile, cov_ref, rows_ref, out_ref, buf, acc, in_sem, cov_sem, out_sem):
     row, col = at_ref[0], at_ref[1]
 
-    def load(g):
-        return pltpu.make_async_copy(rows_ref.at[g], buf.at[g], in_sem.at[g])
+    def load(k):
+        lanes = pl.ds(pl.multiple_of(k // 4 * NB, NB), NB)
+        return pltpu.make_async_copy(rows_ref.at[k % 4, :, lanes], buf.at[k], in_sem.at[k])
 
     def base(k):
         return pltpu.make_async_copy(cov_ref.at[k], acc.at[k], cov_sem.at[k])
@@ -214,50 +215,46 @@
     def store(k):
         return pltpu.make_async_copy(acc.at[k], out_ref.at[k], out_sem.at[k])
 
-    def fetch(g):
-        load(g).start()
-        base(g).start()
-        base(g + 4).start()
+    def fetch(k):
+        load(k).start()
+        base(k).start()
 
     fetch(0)
-
-    def step(g, carry):
-        load(g).wait()
-        base(g).wait()
-        base(g + 4).wait()
-
-        @pl.when(g < 3)
+    fetch(1)
+
+    def step(k, carry):
+        load(k).wait()
+        base(k).wait()
+
+        @pl.when(k < 6)
         def _():
-            fetch(g + 1)
+            fetch(k + 2)
 
         over = (TURN, ((), ()))
-        for l in range(2):
-            k = l * 4 + g
-            rows = buf[g, :, l * NB : (l + 1) * NB]
-            hi = rows.astype(jnp.bfloat16)
-            lo = (rows - hi.astype(F32)).astype(jnp.bfloat16)
-            both = lax.dot_general(hi, split[...], over, preferred_element_type=F32)
-            small = lax.dot_general(lo, split[:, : 2 * NB], over, preferred_element_type=F32)
-            product = both[:, : 2 * NB] + (both[:, 2 * NB :] + small)
-            for q in range(4):
-                place = pl.ds(q, NB, stride=4)
-                at = (q % 2) * NB + (q // 2) * 128
-                left = acc[k, place, :]
-                if q % 2 == 0:
-                    left = jnp.where(col < PANELS, 0.0, left)
-                acc[k, place, :] = left - product[:, at : at + 128]
-
-        @pl.when((g == 0) & (row < PANELS))
+        rows = buf[k]
+        hi = rows.astype(jnp.bfloat16)
+        lo = (rows - hi.astype(F32)).astype(jnp.bfloat16)
+        both = lax.dot_general(hi, split[...], over, preferred_element_type=F32)
+        small = lax.dot_general(lo, split[:, : 2 * NB], over, preferred_element_type=F32)
+        product = both[:, : 2 * NB] + (both[:, 2 * NB :] + small)
+        for q in range(4):
+            place = pl.ds(q, NB, stride=4)
+            at = (q % 2) * NB + (q // 2) * 128
+            left = acc[k, place, :]
+            if q % 2 == 0:
+                left = jnp.where(col < PANELS, 0.0, left)
+            acc[k, place, :] = left - product[:, at : at + 128]
+
+        @pl.when((k == 0) & (row < PANELS))
         def _():
             for part in range(2):
                 acc[0, pl.ds(2 * part, NB, stride=4), :] = tile[:, part * 128 : part * 128 + 128]
                 acc[0, pl.ds(2 * part + 1, NB, stride=4), :] = jnp.zeros((NB, 128), F32)
 
-        store(g).start()
-        store(g + 4).start()
+        store(k).start()
         return carry
 
-    lax.fori_loop(0, 4, step, 0)
+    lax.fori_loop(0, 8, step, 0)
     for k in range(8):
         store(k).wait()
 
@@ -271,9 +268,9 @@
         out_specs=hbm,
         out_shape=jax.ShapeDtypeStruct((8, 4 * NB, 128), F32),
         scratch_shapes=[
-            pltpu.VMEM((4, K, 2 * NB), F32),
+            pltpu.VMEM((8, K, NB), F32),
             pltpu.VMEM((8, 4 * NB, 128), F32),
-            pltpu.SemaphoreType.DMA((4,)),
+            pltpu.SemaphoreType.DMA((8,)),
             pltpu.SemaphoreType.DMA((8,)),
             pltpu.SemaphoreType.DMA((8,)),
         ],

time: 145 us -> 145 us (level)
  no operation moved by 1% of the time
where the time goes in v4:
time: 145 us; the launch traced here: 144 us
  Pallas kernels  45.2 us (31%)
  waiting for transfers between devices  44.8 us (31%)
  starting transfers between devices  37.2 us (26%)
  between operations  13.7 us (9%)
  local copies, waits for them, and re-layouts  3.18 us (2%)
    pallas_call x1, Pallas kernels, factor(): pl.pallas_call(factor_kernel, in_specs=[pl.BlockSpec(memory_space=pltpu.S...  35.5 us
    ppermute x3, waiting for transfers between devices, gather_row(): lax.ppermute(block, 'row', row_perm(s))  19.6 us
    ppermute x3, starting transfers between devices, shards(): got = lax.ppermute(part, 'col', z_perm(step))  11.8 us
    pallas_call x1, Pallas kernels, update(): pl.pallas_call(update_kernel, in_specs=[pl.BlockSpec(memory_space=pltpu.S...  9.69 us
    all_to_all x1, waiting for transfers between devices, shards(): piece = lax.all_to_all(top, 'row', 0, 0, tiled=True)[:K // 8]  9.42 us
    ppermute x3, starting transfers between devices, shards(): lax.ppermute(part, 'col', x_perm(s, PANELS))  7.41 us
    all_to_all x1, starting transfers between devices, shards(): piece = lax.all_to_all(top, 'row', 0, 0, tiled=True)[:K // 8]  6.64 us
    ppermute x3, starting transfers between devices, gather_row(): lax.ppermute(block, 'row', row_perm(s))  6.1 us
  transfers between devices with their start and end apart: 13, of which 9 were waited for; matrix products, arithmetic and copies ran while one was open for 0% of the time, Pallas kernels for 25%

profile of v4, /device:TPU:1, one launch (start us, length us, event | category | flops | bytes accessed | tf_op | source)
XLA Modules:
  0.0 144.4 jit_solution(7577769696082209658)
XLA Ops:
  6.5 1.2 slice.52
  7.8 1.2 all_to_all.8
  9.0 6.6 %all-to-all-start = ((f32[8,32,512]{2,1,0:T(8,128)}), f32[8,32,512]{2,1,0:T(8,128)S(1)}, u32[]{:S(2)}, u32[]{:S(2)}) async-start(f32[8,32,512]{2,1,0:T(8,128)} %all_to_all.8), calls=%async_computation | async-start | bytes 1048576 | tf_op jit(solution)/shard_map/all_to_all | solution.py:318
  15.6 0.0 all-gather.3.cloned.1.call-start
  15.6 0.1 pad_add_fusion.at_ref
  15.7 9.4 %all-to-all-done = f32[8,32,512]{2,1,0:T(8,128)S(1)} async-done(((f32[8,32,512]{2,1,0:T(8,128)}), f32[8,32,512]{2,1,0:T(8,128)S(1)}, u32[]{:S(2)}, u32[]{:S(2)}) %all-to-all-start) | async-done | bytes 524320 | tf_op jit(solution)/shard_map/all_to_all | solution.py:318
  25.1 8.1 %collective-permute-start = (f32[96,256]{1,0:T(8,128)S(1)}, f32[96,256]{1,0:T(8,128)S(1)}, u32[]{:S(2)}, u32[]{:S(2)}) collective-permute-start(f32[96,256]{1,0:T(8,128)S(1)} %slice.68), channel_id=1, source_target_pairs={{0,16},{1,17},{2,18},{32,48},{33,49},{34,50},{64,80},{65,81},{66,8... | collective-permute-start | bytes 294920 | tf_op jit(solution)/shard_map/ppermute | solution.py:323
  33.3 4.2 %collective-permute-start.10 = (f32[96,512]{1,0:T(8,128)S(1)}, f32[96,512]{1,0:T(8,128)S(1)}, u32[]{:S(2)}, u32[]{:S(2)}) collective-permute-start(f32[96,512]{1,0:T(8,128)S(1)} %bitcast.36), channel_id=1, source_target_pairs={{0,0},{1,33},{2,66},{3,99},{4,132},{5,165},{6,198},{7,231},{8,8},{... | collective-permute-start | bytes 589832 | tf_op jit(solution)/shard_map/ppermute | solution.py:320
  37.5 0.0 collective-permute-done
  37.5 2.6 %collective-permute-done.10 = f32[96,512]{1,0:T(8,128)S(1)} collective-permute-done((f32[96,512]{1,0:T(8,128)S(1)}, f32[96,512]{1,0:T(8,128)S(1)}, u32[]{:S(2)}, u32[]{:S(2)}) %collective-permute-start.10) | collective-permute-done | bytes 196640 | tf_op jit(solution)/shard_map/ppermute | solution.py:320
  40.1 0.0 copy-start
  40.1 0.7 copy-done
  40.8 0.0 all-gather.3.cloned.1.call-update
  40.8 1.3 collective-permute-start.1
  42.1 1.6 %collective-permute-done.1 = f32[96,256]{1,0:T(8,128)S(1)} collective-permute-done((f32[96,256]{1,0:T(8,128)S(1)}, f32[96,256]{1,0:T(8,128)S(1)}, u32[]{:S(2)}, u32[]{:S(2)}) %collective-permute-start.1) | collective-permute-done | bytes 98336 | tf_op jit(solution)/shard_map/ppermute | solution.py:323
  43.7 2.4 %collective-permute-start.2 = (f32[96,256]{1,0:T(8,128)S(1)}, f32[96,256]{1,0:T(8,128)S(1)}, u32[]{:S(2)}, u32[]{:S(2)}) collective-permute-start(f32[96,256]{1,0:T(8,128)S(1)} %broadcast_select_fusion.1), channel_id=1, source_target_pairs={{0,4},{1,5},{2,6},{8,12},{9,13},{10,14},{16,20},{17,21},{18,22},{2... | collective-permute-start | bytes 294920 | tf_op jit(solution)/shard_map/ppermute | solution.py:323
  46.1 1.6 %collective-permute-done.2 = f32[96,256]{1,0:T(8,128)S(1)} collective-permute-done((f32[96,256]{1,0:T(8,128)S(1)}, f32[96,256]{1,0:T(8,128)S(1)}, u32[]{:S(2)}, u32[]{:S(2)}) %collective-permute-start.2) | collective-permute-done | bytes 98336 | tf_op jit(solution)/shard_map/ppermute | solution.py:323
  47.7 1.9 %collective-permute-start.5 = (f32[96,256]{1,0:T(8,128)S(1)}, f32[96,256]{1,0:T(8,128)S(1)}, u32[]{:S(2)}, u32[]{:S(2)}) collective-permute-start(f32[96,256]{1,0:T(8,128)S(1)} %broadcast_select_fusion.2), channel_id=1, source_target_pairs={{0,3},{1,0},{2,1},{4,7},{5,4},{6,5},{8,11},{9,8},{10,9},{12,15},{1... | collective-permute-start | bytes 294920 | tf_op jit(solution)/shard_map/ppermute | solution.py:329
  49.7 4.2 %collective-permute-start.4 = (f32[96,256]{1,0:T(8,128)S(1)}, f32[96,256]{1,0:T(8,128)S(1)}, u32[]{:S(2)}, u32[]{:S(2)}) collective-permute-start(f32[96,256]{1,0:T(8,128)S(1)} %broadcast_select_fusion.2), channel_id=1, source_target_pairs={{0,2},{1,3},{2,0},{4,6},{5,7},{6,4},{8,10},{9,11},{10,8},{12,14},{... | collective-permute-start | bytes 294920 | tf_op jit(solution)/shard_map/ppermute | solution.py:329
  53.9 1.3 collective-permute-start.3
  55.2 0.0 collective-permute-done.5
  55.2 2.4 %collective-permute-done.4 = f32[96,256]{1,0:T(8,128)S(1)} collective-permute-done((f32[96,256]{1,0:T(8,128)S(1)}, f32[96,256]{1,0:T(8,128)S(1)}, u32[]{:S(2)}, u32[]{:S(2)}) %collective-permute-start.4) | collective-permute-done | bytes 98336 | tf_op jit(solution)/shard_map/ppermute | solution.py:329
  57.6 0.0 collective-permute-done.3
  57.8 5.4 %collective-permute-start.8 = (f32[32,3072]{1,0:T(8,128)S(1)}, f32[32,3072]{1,0:T(8,128)S(1)}, u32[]{:S(2)}, u32[]{:S(2)}) collective-permute-start(f32[32,3072]{1,0:T(8,128)S(1)} %fusion), channel_id=1, source_target_pairs={{0,192},{32,224},{64,0},{96,32},{128,64},{160,96},{192,128},{224,1... | collective-permute-start | bytes 1179656 | tf_op jit(solution)/shard_map/ppermute | solution.py:304
  63.2 0.0 collective-permute-start.7
  63.2 0.7 collective-permute-start.6
  63.9 14.9 %collective-permute-done.8 = f32[32,3072]{1,0:T(8,128)S(1)} collective-permute-done((f32[32,3072]{1,0:T(8,128)S(1)}, f32[32,3072]{1,0:T(8,128)S(1)}, u32[]{:S(2)}, u32[]{:S(2)}) %collective-permute-start.8) | collective-permute-done | bytes 393248 | tf_op jit(solution)/shard_map/ppermute | solution.py:304
  78.7 0.0 collective-permute-done.7
  78.7 4.8 %collective-permute-done.6 = f32[32,3072]{1,0:T(8,128)S(1)} collective-permute-done((f32[32,3072]{1,0:T(8,128)S(1)}, f32[32,3072]{1,0:T(8,128)S(1)}, u32[]{:S(2)}, u32[]{:S(2)}) %collective-permute-start.6) | collective-permute-done | bytes 393248 | tf_op jit(solution)/shard_map/ppermute | solution.py:304
  83.5 0.1 pad_maximum_fusion.da_ref
  83.6 1.1 collective-permute-start.9
  84.7 3.0 %collective-permute-done.9.db_ref = f32[4,32,3072]{2,1,0:T(8,128)S(1)} collective-permute-done((f32[4,32,3072]{2,1,0:T(8,128)S(1)}, f32[4,32,3072]{2,1,0:T(8,128)S(1)}, u32[]{:S(2)}, u32[]{:S(2)}) %collective-permute-start.9) | collective-permute-done | bytes 1572896 | tf_op jit(solution)/shard_map/ppermute | solution.py:338
  87.8 35.5 %factor.1 = (bf16[768,1024]{1,0:T(8,128)(2,1)S(1)}, f32[256,256]{1,0:T(8,128)S(1)}) custom-call(s32[2]{0:T(128)S(1)} %pad_add_fusion.at_ref, f32[4,32,3072]{2,1,0:T(8,128)S(1)} %pad_maximum_fusion.da_ref, f32[4,32,3072]{2,1,0:T(8,128)S(1)} %collective-permute-done.9.db_ref), custom_call_target="tpu_custom_call" | custom-call | flops 4000000000 | bytes 10000000 | tf_op jit(solution)/shard_map/factor/pallas_call | solution.py:185
  123.3 4.5 %all-gather.3.cloned.1.call-done = f32[3072,512]{1,0:T(8,128)} async-done(((f32[96,512]{1,0:T(8,128)}), f32[3072,512]{1,0:T(8,128)}) %all-gather.3.cloned.1.call-update) | async-done | bytes 6291472 | tf_op jit(solution)/shard_map/all_gather | solution.py:327
  127.8 9.7 %update.1 = f32[8,1024,128]{2,1,0:T(8,128)} custom-call(s32[2]{0:T(128)S(1)} %pad_add_fusion.at_ref, bf16[768,1024]{1,0:T(8,128)(2,1)S(1)} %get-tuple-element.10.split, f32[256,256]{1,0:T(8,128)S(1)} %get-tuple-element.11.tile, f32[8,1024,128]{2,1,0:T(8,128)} %bitcast.37, f32[4,768,512]{2,1,0:T(8,128)} %bitcast.38), custom_call_target="tpu_custom_call" | custom-call | flops 5000000000 | bytes 16000000 | tf_op jit(solution)/shard_map/update/pallas_call | solution.py:265
  (15 shorter events, 0.1 us)
Async XLA Ops:
  9.0 16.1 %all-to-all-start = ((f32[8,32,512]{2,1,0:T(8,128)}), f32[8,32,512]{2,1,0:T(8,128)S(1)}, u32[]{:S(2)}, u32[]{:S(2)}) async-start(f32[8,32,512]{2,1,0:T(8,128)} %all_to_all.8), calls=%async_computation | async-start | bytes 1048576 | tf_op jit(solution)/shard_map/all_to_all | solution.py:318
  15.6 112.2 %all-gather.3.cloned.1.call-start = ((), (), s32[]{:S(2)}) async-start(), calls=%async_computation.1 | async-start | bytes 6488064 | tf_op jit(solution)/shard_map/all_gather | solution.py:327
  25.1 12.4 %collective-permute-start = (f32[96,256]{1,0:T(8,128)S(1)}, f32[96,256]{1,0:T(8,128)S(1)}, u32[]{:S(2)}, u32[]{:S(2)}) collective-permute-start(f32[96,256]{1,0:T(8,128)S(1)} %slice.68), channel_id=1, source_target_pairs={{0,16},{1,17},{2,18},{32,48},{33,49},{34,50},{64,80},{65,81},{66,8... | collective-permute-start | bytes 294920 | tf_op jit(solution)/shard_map/ppermute | solution.py:323
  33.3 6.8 %collective-permute-start.10 = (f32[96,512]{1,0:T(8,128)S(1)}, f32[96,512]{1,0:T(8,128)S(1)}, u32[]{:S(2)}, u32[]{:S(2)}) collective-permute-start(f32[96,512]{1,0:T(8,128)S(1)} %bitcast.36), channel_id=1, source_target_pairs={{0,0},{1,33},{2,66},{3,99},{4,132},{5,165},{6,198},{7,231},{8,8},{... | collective-permute-start | bytes 589832 | tf_op jit(solution)/shard_map/ppermute | solution.py:320
  40.1 0.7 copy-start
  40.8 2.9 %collective-permute-start.1 = (f32[96,256]{1,0:T(8,128)S(1)}, f32[96,256]{1,0:T(8,128)S(1)}, u32[]{:S(2)}, u32[]{:S(2)}) collective-permute-start(f32[96,256]{1,0:T(8,128)S(1)} %broadcast_select_fusion), channel_id=1, source_target_pairs={{0,8},{1,9},{2,10},{16,24},{17,25},{18,26},{32,40},{33,41},{34,42}... | collective-permute-start | bytes 294920 | tf_op jit(solution)/shard_map/ppermute | solution.py:323
  43.7 4.0 %collective-permute-start.2 = (f32[96,256]{1,0:T(8,128)S(1)}, f32[96,256]{1,0:T(8,128)S(1)}, u32[]{:S(2)}, u32[]{:S(2)}) collective-permute-start(f32[96,256]{1,0:T(8,128)S(1)} %broadcast_select_fusion.1), channel_id=1, source_target_pairs={{0,4},{1,5},{2,6},{8,12},{9,13},{10,14},{16,20},{17,21},{18,22},{2... | collective-permute-start | bytes 294920 | tf_op jit(solution)/shard_map/ppermute | solution.py:323
  47.7 7.5 %collective-permute-start.5 = (f32[96,256]{1,0:T(8,128)S(1)}, f32[96,256]{1,0:T(8,128)S(1)}, u32[]{:S(2)}, u32[]{:S(2)}) collective-permute-start(f32[96,256]{1,0:T(8,128)S(1)} %broadcast_select_fusion.2), channel_id=1, source_target_pairs={{0,3},{1,0},{2,1},{4,7},{5,4},{6,5},{8,11},{9,8},{10,9},{12,15},{1... | collective-permute-start | bytes 294920 | tf_op jit(solution)/shard_map/ppermute | solution.py:329
  49.7 7.9 %collective-permute-start.4 = (f32[96,256]{1,0:T(8,128)S(1)}, f32[96,256]{1,0:T(8,128)S(1)}, u32[]{:S(2)}, u32[]{:S(2)}) collective-permute-start(f32[96,256]{1,0:T(8,128)S(1)} %broadcast_select_fusion.2), channel_id=1, source_target_pairs={{0,2},{1,3},{2,0},{4,6},{5,7},{6,4},{8,10},{9,11},{10,8},{12,14},{... | collective-permute-start | bytes 294920 | tf_op jit(solution)/shard_map/ppermute | solution.py:329
  53.9 3.7 %collective-permute-start.3 = (f32[96,256]{1,0:T(8,128)S(1)}, f32[96,256]{1,0:T(8,128)S(1)}, u32[]{:S(2)}, u32[]{:S(2)}) collective-permute-start(f32[96,256]{1,0:T(8,128)S(1)} %broadcast_select_fusion.2), channel_id=1, source_target_pairs={{0,1},{1,2},{2,3},{4,5},{5,6},{6,7},{8,9},{9,10},{10,11},{12,13},{... | collective-permute-start | bytes 294920 | tf_op jit(solution)/shard_map/ppermute | solution.py:329
  57.8 21.0 %collective-permute-start.8 = (f32[32,3072]{1,0:T(8,128)S(1)}, f32[32,3072]{1,0:T(8,128)S(1)}, u32[]{:S(2)}, u32[]{:S(2)}) collective-permute-start(f32[32,3072]{1,0:T(8,128)S(1)} %fusion), channel_id=1, source_target_pairs={{0,192},{32,224},{64,0},{96,32},{128,64},{160,96},{192,128},{224,1... | collective-permute-start | bytes 1179656 | tf_op jit(solution)/shard_map/ppermute | solution.py:304
  63.2 15.5 %collective-permute-start.7 = (f32[32,3072]{1,0:T(8,128)S(1)}, f32[32,3072]{1,0:T(8,128)S(1)}, u32[]{:S(2)}, u32[]{:S(2)}) collective-permute-start(f32[32,3072]{1,0:T(8,128)S(1)} %fusion), channel_id=1, source_target_pairs={{0,128},{32,160},{64,192},{96,224},{128,0},{160,32},{192,64},{224,... | collective-permute-start | bytes 1179656 | tf_op jit(solution)/shard_map/ppermute | solution.py:304
  63.2 20.3 %collective-permute-start.6 = (f32[32,3072]{1,0:T(8,128)S(1)}, f32[32,3072]{1,0:T(8,128)S(1)}, u32[]{:S(2)}, u32[]{:S(2)}) collective-permute-start(f32[32,3072]{1,0:T(8,128)S(1)} %fusion), channel_id=1, source_target_pairs={{0,64},{32,96},{64,128},{96,160},{128,192},{160,224},{192,0},{224,... | collective-permute-start | bytes 1179656 | tf_op jit(solution)/shard_map/ppermute | solution.py:304
  83.6 4.2 %collective-permute-start.9 = (f32[4,32,3072]{2,1,0:T(8,128)S(1)}, f32[4,32,3072]{2,1,0:T(8,128)S(1)}, u32[]{:S(2)}, u32[]{:S(2)}) collective-permute-start(f32[4,32,3072]{2,1,0:T(8,128)S(1)} %pad_maximum_fusion.da_ref), channel_id=1, source_target_pairs={{0,32},{32,0},{64,96},{96,64},{128,160},{160,128},{192,224},{224,1... | collective-permute-start | bytes 4718600 | tf_op jit(solution)/shard_map/ppermute | solution.py:338
Sparse Core Ops, SparseCore 0:
  40.9 86.8 all-gather.2
